TPU v7x, 256 devices: a whole 4x4x8 slice. The times are simulated.
256 devices in a mesh: row: 8 (over x, y_lo), col: 16 (over z, core), ch: 2 (over y_hi).
Axes of the slice: x: 4, y: 4 (y_hi: 2, y_lo: 2; y = y_hi * 2 + y_lo), z: 8, core: 2. Of those that a mesh axis runs over, the one named last changes fastest.
Arguments:
- tokens: bfloat16 [64, 256, 512], P('row', 'col'), may hold values from -6 to 6
- grad_output: bfloat16 [64, 256, 512], P('row', 'col'), may hold values from -6 to 6
- attn_gain: float32 [512], replicated, may hold values from 0.25 to 1.75
- mlp_gain: float32 [512], replicated, may hold values from 0.25 to 1.75
- w_qkv: bfloat16 [512, 3, 512], P(None, None, 'ch'), may hold values from -0.25 to 0.25
- w_out: bfloat16 [512, 512], P('ch'), may hold values from -0.25 to 0.25
- w_up: bfloat16 [512, 2, 2048], P(None, None, 'ch'), may hold values from -0.25 to 0.25
- w_down: bfloat16 [2048, 512], P('ch'), may hold values from -0.125 to 0.125
- head_scale: float32 [8], P('ch'), may hold values from 3 to 120, as said below
Outputs:
- out: bfloat16 [64, 256, 512], P('row', 'col')
- grad_input: bfloat16 [64, 256, 512], P('row', 'col')
- grad_qkv: bfloat16 [512, 3, 512], P(('row', 'col'), None, 'ch')
- grad_out_t: bfloat16 [512, 512], P(('row', 'col'), 'ch')
- grad_up: bfloat16 [512, 2, 2048], P(('row', 'col'), None, 'ch')
- grad_down_t: bfloat16 [512, 2048], P(('row', 'col'), 'ch')
Inputs may be any that keep to these rules, and one draw needn't show every extreme that they name: `head_scale`: positive per-head score scale.
All inputs are finite; a program needn't handle non-finite values.
Results may differ from a plain program's by a relative error of at most 0.03.
The roundings to bfloat16 on the way count: a program that leaves them out, or rounds other values in their place, can miss the bound.
Values may be sent and summed in bfloat16 or wider, within the bound.
A program may use at most 128 MiB of HBM per device.

v0:
```python
import jax
import jax.numpy as jnp
from jax import lax
from jax.sharding import PartitionSpec as P

HEADS = 8
RADIUS = 7


eps = 1e-06


def passed_along(shard, axis, by):
    peers = lax.axis_size(axis)
    pairs = [(i, i + by) for i in range(peers) if 0 <= i + by < peers]
    return lax.ppermute(shard, axis, pairs)


def with_halo(cells, sides, width):
    for axis, dim in sides:
        count = lax.axis_size(axis)
        ends = count - 1
        head = lax.slice_in_dim(cells, 0, width, axis=dim)
        tail = lax.slice_in_dim(cells, cells.shape[dim] - width, cells.shape[dim], axis=dim)
        cells = jnp.concatenate(
            [
                lax.ppermute(tail, axis, [(i, (i + 1) % count) for i in range(ends)]),
                cells,
                lax.ppermute(head, axis, [((i + 1) % count, i) for i in range(ends)]),
            ],
            axis=dim,
        )
    return cells


def normalize(values, gain):
    scale = lax.rsqrt(jnp.mean(values * values, axis=-1, keepdims=True) + eps)
    return values * scale * gain


def normalize_back(values, gain, upstream):
    scale = lax.rsqrt(jnp.mean(values * values, axis=-1, keepdims=True) + eps)
    normed = values * scale
    incoming = upstream * gain
    return scale * (incoming - normed * jnp.mean(incoming * normed, axis=-1, keepdims=True))


def gelu_parts(gate):
    cdf = 0.5 * (1.0 + jax.scipy.special.erf(gate * 0.7071067811865476))
    density = jnp.exp(-0.5 * gate * gate) * 0.3989422804014327
    return (gate * cdf, cdf + gate * density)


def allowed_mask(inside, rows, cols, radius):
    spans = inside.shape[0] - rows + 1
    stacked = jnp.stack([inside[offset : offset + rows] for offset in range(spans)], axis=1)
    inside_rows = jnp.transpose(stacked, (1, 2, 0))
    key_col = jnp.arange(cols + 2 * radius, dtype=jnp.int32)[:, None]
    query_col = jnp.arange(cols, dtype=jnp.int32)[None, :]
    band = (key_col - query_col >= 0) & (key_col - query_col <= 2 * radius)
    return inside_rows[:, :, :, None] & band[None, :, None, :]


def pair_scores(left_grid, window, rows, spans):
    return jnp.stack(
        [
            jnp.einsum(
                "rchd,rkhd->hkrc",
                left_grid,
                window[offset : offset + rows],
                preferred_element_type=jnp.float32,
            )
            for offset in range(spans)
        ],
        axis=1,
    )


def mix_window(factors, window, rows, spans):
    total = None
    for offset in range(spans):
        term = jnp.einsum(
            "hkrc,rkhd->rchd",
            factors[:, offset],
            window[offset : offset + rows],
            preferred_element_type=jnp.float32,
        )
        total = term if total is None else total + term
    return total


def spread_window(factors, grid, spans):
    total = None
    for offset in range(spans):
        term = jnp.einsum(
            "hkrc,rchd->rkhd", factors[:, offset], grid, preferred_element_type=jnp.float32
        )
        term = jnp.pad(term, ((offset, spans - 1 - offset), (0, 0), (0, 0), (0, 0)))
        total = term if total is None else total + term
    return total


def softmax_masked(scores, allowed):
    scores = jnp.where(allowed, scores, -1e30)
    highest = jnp.max(scores, axis=(1, 2), keepdims=True)
    raised = jnp.where(allowed, jnp.exp(scores - highest), 0.0)
    return raised / jnp.sum(raised, axis=(1, 2), keepdims=True)


def through_norm(raw, norm, incoming, factor):
    along = jnp.sum(raw * incoming, axis=-1, keepdims=True)
    return factor * norm * (incoming - norm * norm * raw * along)


def contract_cols(left, right):
    return lax.dot_general(
        left, right, (((1,), (1,)), ((), ())), preferred_element_type=jnp.float32
    )


def outer_rows(left, right):
    return lax.dot_general(
        left, right, (((0,), (0,)), ((), ())), preferred_element_type=jnp.float32
    )


def channel_total(partial_value):
    return lax.psum(partial_value.astype(jnp.bfloat16), "ch").astype(jnp.float32)


def send_cols(block, offset):
    return passed_along(block.astype(jnp.bfloat16), "col", offset).astype(block.dtype)


def send_rows(block, offset):
    return passed_along(block.astype(jnp.bfloat16), "row", offset).astype(block.dtype)


def return_rims(padded, radius, rows, cols):
    edge = 2 * radius
    from_right = send_cols(padded[:, :radius], -1)
    from_left = send_cols(padded[:, cols + radius :], 1)
    padded = padded.at[:, cols : cols + radius].add(from_right)
    padded = padded.at[:, radius:edge].add(from_left)
    middle = padded[:, radius : cols + radius]
    from_below = send_rows(middle[:radius], -1)
    from_above = send_rows(middle[rows + radius :], 1)
    middle = middle.at[rows : rows + radius].add(from_below)
    middle = middle.at[radius:edge].add(from_above)
    return middle[radius : rows + radius]


def shards(tokens, grad_output, attn_gain, mlp_gain, w_qkv, w_out, w_up, w_down, head_scale):
    rows, cols, width = tokens.shape
    heads_here = head_scale.shape[0]
    head_dim = width // HEADS
    inner = heads_here * head_dim
    count = rows * cols
    hidden_here = w_down.shape[0]
    radius = RADIUS
    edge = 2 * radius
    spans = edge + 1
    flat_in = tokens.reshape(count, width)
    flat_grad = grad_output.reshape(count, width)
    devices = lax.axis_size("row") * lax.axis_size("col")
    slice_rows = width // devices

    def settle(partial_value):
        return channel_total(partial_value)

    attn_in = normalize(flat_in.astype(jnp.float32), attn_gain).astype(jnp.bfloat16)
    projected = jnp.dot(
        attn_in, w_qkv.reshape(width, 3 * inner), preferred_element_type=jnp.float32
    )
    projected = projected.reshape(count, 3, heads_here, head_dim)
    query_raw = projected[:, 0]
    key_raw = projected[:, 1]
    query_norm = lax.rsqrt(jnp.sum(query_raw * query_raw, axis=-1, keepdims=True) + eps)
    key_norm = lax.rsqrt(jnp.sum(key_raw * key_raw, axis=-1, keepdims=True) + eps)
    scale = head_scale[:, None]
    queries = (query_raw * query_norm * scale).astype(jnp.bfloat16)
    keys = (key_raw * key_norm).astype(jnp.bfloat16)
    values = projected[:, 2].astype(jnp.bfloat16)
    paired = jnp.stack([keys, values], axis=1).reshape(rows, cols, 2 * inner)
    window = with_halo(paired, (("row", 0), ("col", 1)), radius)
    window = window.reshape(rows + edge, cols + edge, 2, heads_here, head_dim)
    key_window = window[:, :, 0]
    value_window = window[:, :, 1]
    row_ids = lax.axis_index("row") * rows - radius + jnp.arange(rows + edge, dtype=jnp.int32)
    col_ids = lax.axis_index("col") * cols - radius + jnp.arange(cols + edge, dtype=jnp.int32)
    row_inside = (row_ids >= 0) & (row_ids < rows * lax.axis_size("row"))
    col_inside = (col_ids >= 0) & (col_ids < cols * lax.axis_size("col"))
    allowed = allowed_mask(row_inside[:, None] & col_inside[None, :], rows, cols, radius)
    query_grid = queries.reshape(rows, cols, heads_here, head_dim)
    weights = softmax_masked(pair_scores(query_grid, key_window, rows, spans), allowed)
    weights_low = weights.astype(jnp.bfloat16)
    attended = mix_window(weights_low, value_window, rows, spans)
    attended = attended.astype(jnp.bfloat16).reshape(count, inner)
    attn_part = jnp.dot(attended, w_out, preferred_element_type=jnp.float32)
    residual = flat_in.astype(jnp.float32) + settle(attn_part)
    mlp_in = normalize(residual, mlp_gain).astype(jnp.bfloat16)
    mixed = jnp.dot(
        mlp_in, w_up.reshape(width, 2 * hidden_here), preferred_element_type=jnp.float32
    )
    mixed = mixed.reshape(count, 2, hidden_here)
    gate = mixed[:, 0]
    value_part = mixed[:, 1]
    activated, slope = gelu_parts(gate)
    hidden = (activated * value_part).astype(jnp.bfloat16)
    mlp_part = jnp.dot(hidden, w_down, preferred_element_type=jnp.float32)
    out = (residual + settle(mlp_part)).astype(jnp.bfloat16)
    grad_hidden = contract_cols(flat_grad, w_down)
    grad_mix = jnp.stack(
        [grad_hidden * value_part * slope, grad_hidden * activated], axis=1
    ).astype(jnp.bfloat16)
    grad_mix = grad_mix.reshape(count, 2 * hidden_here)
    grad_mlp_part = contract_cols(grad_mix, w_up.reshape(width, 2 * hidden_here))
    grad_resid = flat_grad.astype(jnp.float32) + normalize_back(
        residual, mlp_gain, settle(grad_mlp_part)
    )
    grad_resid_low = grad_resid.astype(jnp.bfloat16)
    grad_attended = contract_cols(grad_resid_low, w_out).astype(jnp.bfloat16)
    grad_grid = grad_attended.reshape(rows, cols, heads_here, head_dim)
    grad_weights = pair_scores(grad_grid, value_window, rows, spans)
    delta = jnp.sum(weights * grad_weights, axis=(1, 2), keepdims=True)
    grad_scores = (weights * (grad_weights - delta)).astype(jnp.bfloat16)
    grad_query_hat = mix_window(grad_scores, key_window, rows, spans)
    grad_key_win = spread_window(grad_scores, query_grid, spans)
    grad_value_win = spread_window(weights_low, grad_grid, spans)
    rims = jnp.stack([grad_key_win, grad_value_win], axis=2).reshape(
        rows + edge, cols + edge, 2 * inner
    )
    owned = return_rims(rims, radius, rows, cols).reshape(count, 2, heads_here, head_dim)
    grad_query_raw = through_norm(
        query_raw, query_norm, grad_query_hat.reshape(count, heads_here, head_dim), scale
    )
    grad_key_raw = through_norm(key_raw, key_norm, owned[:, 0], 1.0)
    grad_proj = jnp.stack([grad_query_raw, grad_key_raw, owned[:, 1]], axis=1).astype(jnp.bfloat16)
    grad_proj = grad_proj.reshape(count, 3 * inner)
    grad_attn_part = contract_cols(grad_proj, w_qkv.reshape(width, 3 * inner))
    grad_in = grad_resid + normalize_back(
        flat_in.astype(jnp.float32), attn_gain, settle(grad_attn_part)
    )
    grad_input = grad_in.astype(jnp.bfloat16)
    reduced = lax.psum_scatter(
        jnp.concatenate(
            [
                outer_rows(attn_in, grad_proj),
                jnp.concatenate(
                    [
                        outer_rows(mlp_in, grad_mix),
                        outer_rows(grad_resid_low, attended),
                        outer_rows(flat_grad, hidden),
                    ],
                    axis=1,
                ),
            ],
            axis=1,
        ),
        ("row", "col"),
        scatter_dimension=0,
        tiled=True,
    )
    reduced = reduced.astype(jnp.bfloat16)
    first_mark = 3 * inner
    second_mark = first_mark + 2 * hidden_here
    third_mark = second_mark + inner
    grad_qkv = reduced[:, :first_mark].reshape(slice_rows, 3, inner)
    grad_up = reduced[:, first_mark:second_mark].reshape(slice_rows, 2, hidden_here)
    grad_out_t = reduced[:, second_mark:third_mark]
    grad_down_t = reduced[:, third_mark:]
    return (
        out.reshape(rows, cols, width),
        grad_input.reshape(rows, cols, width),
        grad_qkv,
        grad_out_t,
        grad_up,
        grad_down_t,
    )


def solution(mesh):
    placed = (
        P("row", "col", None),
        P("row", "col", None),
        P(),
        P(),
        P(None, None, "ch"),
        P("ch", None),
        P(None, None, "ch"),
        P("ch", None),
        P("ch"),
    )
    return jax.shard_map(
        shards,
        mesh=mesh,
        in_specs=placed,
        out_specs=(
            P("row", "col", None),
            P("row", "col", None),
            P(("row", "col"), None, "ch"),
            P(("row", "col"), "ch"),
            P(("row", "col"), None, "ch"),
            P(("row", "col"), "ch"),
        ),
        check_vma=False,
    )
```

profile of v0, /device:TPU:8, one launch (start us, length us, event | category | flops | bytes accessed | tf_op | source)
XLA Modules:
  0.0 897.4 jit_solution(1358922691232553742)
XLA Ops:
  7.2 1.1 fusion.124
  8.3 1.4 copy.342
  9.8 1.1 fusion.126
  11.4 1.3 broadcast_multiply_fusion
  13.2 3.3 collective-permute-start
  16.8 2.6 collective-permute-start.1
  20.6 3.8 collective-permute-done.1
  24.5 1.3 collective-permute-start.3
  25.8 3.2 collective-permute-start.2
  29.9 1.2 pad_maximum_fusion.2
  31.1 2.6 reshape.368
  34.4 2.2 fusion.256
  41.7 1.3 fusion.1
  43.0 1.2 fusion.255
  48.2 1.8 convolution_convert_fusion.2
  50.9 3.6 copy.590
  54.6 4.0 copy.393
  59.7 31.5 %all-reduce.37.cloned.1.call-done = bf16[128,512]{1,0:T(8,128)(2,1)} async-done(((bf16[128,512]{1,0:T(8,128)(2,1)}), bf16[128,512]{1,0:T(8,128)(2,1)}) %all-reduce.37.cloned.1.call-update) | async-done | bytes 131088 | tf_op jit(solution)/shard_map/psum | solution.py:128
  91.3 1.0 multiply_reduce_fusion.2
  92.3 1.0 multiply_convert_fusion.3
  93.3 2.5 fusion.134
  95.9 1.9 convolution_bitcast_fusion
  99.1 1.6 fusion.39
  100.6 1.9 maximum_convert_fusion
  102.6 2.1 copy.522
  104.7 3.8 fusion.264
  108.5 1.0 convolution_convert_fusion.1
  109.5 27.3 %all-reduce.39.cloned.1.call-done = bf16[128,512]{1,0:T(8,128)(2,1)} async-done(((bf16[128,512]{1,0:T(8,128)(2,1)}), bf16[128,512]{1,0:T(8,128)(2,1)}) %all-reduce.39.cloned.1.call-update) | async-done | bytes 131088 | tf_op jit(solution)/shard_map/psum | solution.py:128
  136.8 1.1 multiply_reduce_fusion.1
  137.9 1.2 multiply_add_fusion
  139.0 1.3 convolution_convert_fusion.3
  140.5 1.2 convolution_bitcast_fusion.1
  141.7 1.2 convolution_bitcast_fusion.2
  142.9 1.2 convolution_bitcast_fusion.3
  151.6 1.7 multiply_reduce_fusion
  153.3 2.1 multiply_convert_fusion
  161.3 1.0 add_bitcast_fusion
  162.3 1.0 add_bitcast_fusion.1
  163.9 3.6 copy.519
  167.5 3.3 reshape.376
  171.8 1.3 collective-permute-start.4
  173.1 3.8 collective-permute-start.5
  177.0 1.3 convolution_add_fusion.13
  178.3 1.1 convolution_add_fusion.12
  182.9 1.1 fusion.198
  184.9 1.4 scatter-add.14
  186.3 1.0 slice_add_fusion
  187.3 1.2 scatter-add.15
  188.8 3.5 collective-permute-start.6
  192.4 3.4 collective-permute-start.7
  195.8 1.4 collective-permute-done.6
  197.3 2.4 collective-permute-done.7
  200.5 2.0 reshape.377
  202.5 1.6 slice.810
  204.2 1.7 slice.809
  205.9 1.6 copy.589
  207.5 1.7 copy.588
  210.2 1.0 multiply_convert_fusion.6
  213.0 1.3 fusion.263
  214.3 5.4 pad_maximum_fusion
  219.8 593.2 %all-reduce.42 = bf16[512,4096]{1,0:T(8,128)(2,1)} all-reduce(f32[512,4096]{1,0:T(8,128)} %pad_maximum_fusion), channel_id=2, replica_groups=mesh['row'=8,'col'=16,'ch'=2] {'row','col'}, use_global_device_ids=true, to_apply=%region_15.16.clone | all-reduce | flops 2097152 | bytes 12582912
  816.3 71.5 %all-reduce.41.cloned.1.call-done = (bf16[128,512]{1,0:T(8,128)(2,1)}, bf16[128,512]{1,0:T(8,128)(2,1)}) async-done(((bf16[128,512]{1,0:T(8,128)(2,1)}, bf16[128,512]{1,0:T(8,128)(2,1)}), (bf16[128,512]{1,0:T(8,128)(2,1)}, bf16[128,512]{1,0:T(8,128)(2,1)})) %all-reduce.41.cloned.1.call-update) | async-done | bytes 262160 | tf_op jit(solution)/shard_map/psum | solution.py:128
  887.8 1.1 fusion.119
  888.9 1.8 fusion.123
  (431 shorter events, 41.0 us)
Async XLA Ops:
  7.2 90.6 %copy-start = (bf16[1024,512]{1,0:T(8,128)(2,1)S(1)}, bf16[1024,512]{1,0:T(8,128)(2,1)}, u32[]{:S(2)}) copy-start(bf16[1024,512]{1,0:T(8,128)(2,1)} %param.24) | copy-start | bytes 3145732
  7.2 12.8 %copy-start.127 = (f32[4]{0:T(128)S(1)}, f32[4]{0:T(128)}, u32[]{:S(2)}) copy-start(f32[4]{0:T(128)} %param.25) | copy-start | bytes 52
  7.2 84.1 %all-reduce.37.cloned.1.call-start = ((), (), s32[]{:S(2)}) async-start(), calls=%async_computation | async-start | bytes 262144 | tf_op jit(solution)/shard_map/psum | solution.py:128
  9.8 19.3 %copy-start.6 = (bf16[512,3,256]{0,2,1:T(8,128)(2,1)}, bf16[512,3,256]{0,2,1:T(8,128)(2,1)S(1)}, u32[]{:S(2)}) copy-start(bf16[512,3,256]{0,2,1:T(8,128)(2,1)S(1)} %copy.342) | copy-start | bytes 2359300
  10.9 9.0 %copy-start.120 = (bf16[8,16,512]{2,1,0:T(8,128)(2,1)}, bf16[8,16,512]{2,1,0:T(8,128)(2,1)S(1)}, u32[]{:S(2)}) copy-start(bf16[8,16,512]{2,1,0:T(8,128)(2,1)S(1)} %fusion.126) | copy-start | bytes 393220
  11.3 180.9 %copy-start.8 = (f32[128,3,4,64]{0,3,2,1:T(8,128)}, f32[128,3,4,64]{0,3,2,1:T(8,128)S(1)}, u32[]{:S(2)}) copy-start(f32[128,3,4,64]{0,3,2,1:T(8,128)S(1)} %fusion.262) | copy-start | bytes 1179652
  13.2 7.4 collective-permute-start
  16.8 7.6 collective-permute-start.1
  24.5 4.7 collective-permute-start.3
  25.8 4.1 collective-permute-start.2
  34.4 10.5 %copy-start.70 = (bf16[8,30,1,4,64]{4,3,2,1,0:T(4,128)(2,1)}, bf16[8,30,1,4,64]{4,3,2,1,0:T(4,128)(2,1)S(1)}, u32[]{:S(2)}) copy-start(bf16[8,30,1,4,64]{4,3,2,1,0:T(4,128)(2,1)S(1)} %get-tuple-element.123) | copy-start | bytes 368644
  34.4 13.2 %copy-start.66 = (bf16[8,30,1,4,64]{4,3,2,1,0:T(4,128)(2,1)}, bf16[8,30,1,4,64]{4,3,2,1,0:T(4,128)(2,1)S(1)}, u32[]{:S(2)}) copy-start(bf16[8,30,1,4,64]{4,3,2,1,0:T(4,128)(2,1)S(1)} %get-tuple-element.113) | copy-start | bytes 368644
  36.8 8.3 copy-start.49
  36.8 8.5 copy-start.47
  36.8 8.7 copy-start.45
  36.8 8.9 copy-start.43
  36.8 9.1 %copy-start.41 = (bf16[8,30,1,4,64]{4,3,2,1,0:T(4,128)(2,1)}, bf16[8,30,1,4,64]{4,3,2,1,0:T(4,128)(2,1)S(1)}, u32[]{:S(2)}) copy-start(bf16[8,30,1,4,64]{4,3,2,1,0:T(4,128)(2,1)S(1)} %get-tuple-element.102) | copy-start | bytes 368644
  36.8 9.3 %copy-start.39 = (bf16[8,30,1,4,64]{4,3,2,1,0:T(4,128)(2,1)}, bf16[8,30,1,4,64]{4,3,2,1,0:T(4,128)(2,1)S(1)}, u32[]{:S(2)}) copy-start(bf16[8,30,1,4,64]{4,3,2,1,0:T(4,128)(2,1)S(1)} %get-tuple-element.101) | copy-start | bytes 368644
  36.8 9.5 %copy-start.37 = (bf16[8,30,1,4,64]{4,3,2,1,0:T(4,128)(2,1)}, bf16[8,30,1,4,64]{4,3,2,1,0:T(4,128)(2,1)S(1)}, u32[]{:S(2)}) copy-start(bf16[8,30,1,4,64]{4,3,2,1,0:T(4,128)(2,1)S(1)} %get-tuple-element.100) | copy-start | bytes 368644
  36.8 9.7 %copy-start.35 = (bf16[8,30,1,4,64]{4,3,2,1,0:T(4,128)(2,1)}, bf16[8,30,1,4,64]{4,3,2,1,0:T(4,128)(2,1)S(1)}, u32[]{:S(2)}) copy-start(bf16[8,30,1,4,64]{4,3,2,1,0:T(4,128)(2,1)S(1)} %get-tuple-element.99) | copy-start | bytes 368644
  36.8 9.9 %copy-start.33 = (bf16[8,30,1,4,64]{4,3,2,1,0:T(4,128)(2,1)}, bf16[8,30,1,4,64]{4,3,2,1,0:T(4,128)(2,1)S(1)}, u32[]{:S(2)}) copy-start(bf16[8,30,1,4,64]{4,3,2,1,0:T(4,128)(2,1)S(1)} %get-tuple-element.98) | copy-start | bytes 368644
  36.8 10.1 %copy-start.31 = (bf16[8,30,1,4,64]{4,3,2,1,0:T(4,128)(2,1)}, bf16[8,30,1,4,64]{4,3,2,1,0:T(4,128)(2,1)S(1)}, u32[]{:S(2)}) copy-start(bf16[8,30,1,4,64]{4,3,2,1,0:T(4,128)(2,1)S(1)} %get-tuple-element.97) | copy-start | bytes 368644
  36.9 10.3 %copy-start.29 = (bf16[8,30,1,4,64]{4,3,2,1,0:T(4,128)(2,1)}, bf16[8,30,1,4,64]{4,3,2,1,0:T(4,128)(2,1)S(1)}, u32[]{:S(2)}) copy-start(bf16[8,30,1,4,64]{4,3,2,1,0:T(4,128)(2,1)S(1)} %get-tuple-element.96) | copy-start | bytes 368644
  36.9 10.5 %copy-start.27 = (bf16[8,30,1,4,64]{4,3,2,1,0:T(4,128)(2,1)}, bf16[8,30,1,4,64]{4,3,2,1,0:T(4,128)(2,1)S(1)}, u32[]{:S(2)}) copy-start(bf16[8,30,1,4,64]{4,3,2,1,0:T(4,128)(2,1)S(1)} %get-tuple-element.95) | copy-start | bytes 368644
  36.9 10.9 %copy-start.25 = (bf16[8,30,1,4,64]{4,3,2,1,0:T(4,128)(2,1)}, bf16[8,30,1,4,64]{4,3,2,1,0:T(4,128)(2,1)S(1)}, u32[]{:S(2)}) copy-start(bf16[8,30,1,4,64]{4,3,2,1,0:T(4,128)(2,1)S(1)} %get-tuple-element.94) | copy-start | bytes 368644
  50.1 86.7 %all-reduce.39.cloned.1.call-start = ((), (), s32[]{:S(2)}) async-start(), calls=%async_computation.1 | async-start | bytes 262144 | tf_op jit(solution)/shard_map/psum | solution.py:128
  50.9 40.3 %copy-start.4 = (bf16[8,16,512]{2,1,0:T(8,128)(2,1)S(1)}, bf16[8,16,512]{2,1,0:T(8,128)(2,1)}, u32[]{:S(2)}) copy-start(bf16[8,16,512]{2,1,0:T(8,128)(2,1)} %param.17) | copy-start | bytes 393220
  50.9 41.3 %copy-start.124 = (f32[512]{0:T(512)S(1)}, f32[512]{0:T(512)}, u32[]{:S(2)}) copy-start(f32[512]{0:T(512)} %param.20) | copy-start | bytes 6148
  54.6 41.3 %copy-start.121 = (bf16[8,16,512]{2,1,0:T(8,128)(2,1)S(1)}, bf16[8,16,512]{2,1,0:T(8,128)(2,1)}, u32[]{:S(2)}) copy-start(bf16[8,16,512]{2,1,0:T(8,128)(2,1)} %param.18) | copy-start | bytes 393220
  102.5 34.3 %copy-start.12 = (bf16[128,512]{1,0:T(8,128)(2,1)S(1)}, bf16[128,512]{1,0:T(8,128)(2,1)}, u32[]{:S(2)}) copy-start(bf16[128,512]{1,0:T(8,128)(2,1)} %all-reduce.37.cloned.1.call-done) | copy-start | bytes 393220
  102.5 785.3 %all-reduce.41.cloned.1.call-start = ((), (), s32[]{:S(2)}) async-start(), calls=%async_computation.2 | async-start | bytes 524288 | tf_op jit(solution)/shard_map/psum | solution.py:128
  108.5 36.5 %copy-start.88 = (bf16[4,30,8,16]{1,3,2,0:T(8,128)(2,1)S(1)}, bf16[4,30,8,16]{1,3,2,0:T(8,128)(2,1)}, u32[]{:S(2)}) copy-start(bf16[4,30,8,16]{1,3,2,0:T(8,128)(2,1)} %copy-done.87) | copy-start | bytes 92164
  109.5 34.6 %copy-start.94 = (bf16[4,30,8,16]{1,3,2,0:T(8,128)(2,1)S(1)}, bf16[4,30,8,16]{1,3,2,0:T(8,128)(2,1)}, u32[]{:S(2)}) copy-start(bf16[4,30,8,16]{1,3,2,0:T(8,128)(2,1)} %copy-done.93) | copy-start | bytes 92164
  109.5 34.9 %copy-start.92 = (bf16[4,30,8,16]{1,3,2,0:T(8,128)(2,1)S(1)}, bf16[4,30,8,16]{1,3,2,0:T(8,128)(2,1)}, u32[]{:S(2)}) copy-start(bf16[4,30,8,16]{1,3,2,0:T(8,128)(2,1)} %copy-done.91) | copy-start | bytes 92164
  109.5 35.2 %copy-start.90 = (bf16[4,30,8,16]{1,3,2,0:T(8,128)(2,1)S(1)}, bf16[4,30,8,16]{1,3,2,0:T(8,128)(2,1)}, u32[]{:S(2)}) copy-start(bf16[4,30,8,16]{1,3,2,0:T(8,128)(2,1)} %copy-done.89) | copy-start | bytes 92164
  109.5 35.8 %copy-start.86 = (bf16[4,30,8,16]{1,3,2,0:T(8,128)(2,1)S(1)}, bf16[4,30,8,16]{1,3,2,0:T(8,128)(2,1)}, u32[]{:S(2)}) copy-start(bf16[4,30,8,16]{1,3,2,0:T(8,128)(2,1)} %copy-done.85) | copy-start | bytes 92164
  139.0 43.9 %copy-start.10 = (f32[128,512]{1,0:T(8,128)}, f32[128,512]{1,0:T(8,128)S(1)}, u32[]{:S(2)}) copy-start(f32[128,512]{1,0:T(8,128)S(1)} %multiply_add_fusion) | copy-start | bytes 786436
  167.5 10.8 %copy-start.64 = (bf16[8,30,1,4,64]{4,3,2,1,0:T(4,128)(2,1)S(1)}, bf16[8,30,1,4,64]{4,3,2,1,0:T(4,128)(2,1)}, u32[]{:S(2)}) copy-start(bf16[8,30,1,4,64]{4,3,2,1,0:T(4,128)(2,1)} %copy-done.63) | copy-start | bytes 368644
  167.5 12.0 %copy-start.62 = (bf16[8,30,1,4,64]{4,3,2,1,0:T(4,128)(2,1)S(1)}, bf16[8,30,1,4,64]{4,3,2,1,0:T(4,128)(2,1)}, u32[]{:S(2)}) copy-start(bf16[8,30,1,4,64]{4,3,2,1,0:T(4,128)(2,1)} %copy-done.61) | copy-start | bytes 368644
  167.5 12.2 %copy-start.60 = (bf16[8,30,1,4,64]{4,3,2,1,0:T(4,128)(2,1)S(1)}, bf16[8,30,1,4,64]{4,3,2,1,0:T(4,128)(2,1)}, u32[]{:S(2)}) copy-start(bf16[8,30,1,4,64]{4,3,2,1,0:T(4,128)(2,1)} %copy-done.59) | copy-start | bytes 368644
  170.8 8.7 copy-start.116
  170.8 8.9 copy-start.114
  170.8 9.1 %copy-start.58 = (bf16[8,30,1,4,64]{4,3,2,1,0:T(4,128)(2,1)S(1)}, bf16[8,30,1,4,64]{4,3,2,1,0:T(4,128)(2,1)}, u32[]{:S(2)}) copy-start(bf16[8,30,1,4,64]{4,3,2,1,0:T(4,128)(2,1)} %copy-done.57) | copy-start | bytes 368644
  170.8 9.1 %copy-start.112 = (bf16[4,30,8,16]{1,3,2,0:T(8,128)(2,1)S(1)}, bf16[4,30,8,16]{1,3,2,0:T(8,128)(2,1)}, u32[]{:S(2)}) copy-start(bf16[4,30,8,16]{1,3,2,0:T(8,128)(2,1)} %copy-done.111) | copy-start | bytes 92164
  170.8 9.3 %copy-start.56 = (bf16[8,30,1,4,64]{4,3,2,1,0:T(4,128)(2,1)S(1)}, bf16[8,30,1,4,64]{4,3,2,1,0:T(4,128)(2,1)}, u32[]{:S(2)}) copy-start(bf16[8,30,1,4,64]{4,3,2,1,0:T(4,128)(2,1)} %copy-done.55) | copy-start | bytes 368644
  170.8 9.3 %copy-start.110 = (bf16[4,30,8,16]{1,3,2,0:T(8,128)(2,1)S(1)}, bf16[4,30,8,16]{1,3,2,0:T(8,128)(2,1)}, u32[]{:S(2)}) copy-start(bf16[4,30,8,16]{1,3,2,0:T(8,128)(2,1)} %copy-done.109) | copy-start | bytes 92164
  170.8 9.5 %copy-start.54 = (bf16[8,30,1,4,64]{4,3,2,1,0:T(4,128)(2,1)S(1)}, bf16[8,30,1,4,64]{4,3,2,1,0:T(4,128)(2,1)}, u32[]{:S(2)}) copy-start(bf16[8,30,1,4,64]{4,3,2,1,0:T(4,128)(2,1)} %copy-done.53) | copy-start | bytes 368644
  170.8 9.5 %copy-start.108 = (bf16[4,30,8,16]{1,3,2,0:T(8,128)(2,1)S(1)}, bf16[4,30,8,16]{1,3,2,0:T(8,128)(2,1)}, u32[]{:S(2)}) copy-start(bf16[4,30,8,16]{1,3,2,0:T(8,128)(2,1)} %copy-done.107) | copy-start | bytes 92164
  171.0 9.6 %copy-start.52 = (bf16[8,30,1,4,64]{4,3,2,1,0:T(4,128)(2,1)S(1)}, bf16[8,30,1,4,64]{4,3,2,1,0:T(4,128)(2,1)}, u32[]{:S(2)}) copy-start(bf16[8,30,1,4,64]{4,3,2,1,0:T(4,128)(2,1)} %copy-done.51) | copy-start | bytes 368644
  171.0 9.6 %copy-start.106 = (bf16[4,30,8,16]{1,3,2,0:T(8,128)(2,1)S(1)}, bf16[4,30,8,16]{1,3,2,0:T(8,128)(2,1)}, u32[]{:S(2)}) copy-start(bf16[4,30,8,16]{1,3,2,0:T(8,128)(2,1)} %copy-done.105) | copy-start | bytes 92164
  171.0 9.8 %copy-start.24 = (bf16[8,30,1,4,64]{4,3,2,1,0:T(4,128)(2,1)S(1)}, bf16[8,30,1,4,64]{4,3,2,1,0:T(4,128)(2,1)}, u32[]{:S(2)}) copy-start(bf16[8,30,1,4,64]{4,3,2,1,0:T(4,128)(2,1)} %copy-done.23) | copy-start | bytes 368644
  171.0 9.8 %copy-start.104 = (bf16[4,30,8,16]{1,3,2,0:T(8,128)(2,1)S(1)}, bf16[4,30,8,16]{1,3,2,0:T(8,128)(2,1)}, u32[]{:S(2)}) copy-start(bf16[4,30,8,16]{1,3,2,0:T(8,128)(2,1)} %copy-done.103) | copy-start | bytes 92164
  171.8 12.2 %collective-permute-start.4 = (bf16[22,7,512]{2,1,0:T(8,128)(2,1)}, bf16[22,7,512]{2,1,0:T(8,128)(2,1)}, u32[]{:S(2)}, u32[]{:S(2)}) collective-permute-start(bf16[22,7,512]{2,1,0:T(8,128)(2,1)} %get-tuple-element.127), channel_id=1, source_target_pairs={{2,0},{4,2},{6,4},{8,6},{10,8},{12,10},{14,12},{16,14},{18,16},{20... | collective-permute-start | bytes 473096 | tf_op jit(solution)/shard_map/ppermute | solution.py:16
  173.1 7.9 copy-start.22
  173.1 13.2 %collective-permute-start.5 = (bf16[22,7,512]{2,1,0:T(8,128)(2,1)}, bf16[22,7,512]{2,1,0:T(8,128)(2,1)}, u32[]{:S(2)}, u32[]{:S(2)}) collective-permute-start(bf16[22,7,512]{2,1,0:T(8,128)(2,1)} %get-tuple-element.126), channel_id=1, source_target_pairs={{0,2},{2,4},{4,6},{6,8},{8,10},{10,12},{12,14},{14,16},{16,18},{18... | collective-permute-start | bytes 473096 | tf_op jit(solution)/shard_map/ppermute | solution.py:16
  188.7 23.4 %copy-start.7 = (bf16[512,3,256]{0,2,1:T(8,128)(2,1)S(1)}, bf16[512,3,256]{0,2,1:T(8,128)(2,1)}, u32[]{:S(2)}) copy-start(bf16[512,3,256]{0,2,1:T(8,128)(2,1)} %copy-done.6) | copy-start | bytes 2359300
  188.8 8.5 collective-permute-start.6
  192.3 16.9 %copy-start.9 = (f32[128,3,4,64]{0,3,2,1:T(8,128)S(1)}, f32[128,3,4,64]{0,3,2,1:T(8,128)}, u32[]{:S(2)}) copy-start(f32[128,3,4,64]{0,3,2,1:T(8,128)} %copy-done.8) | copy-start | bytes 1179652
  192.4 7.3 collective-permute-start.7
  197.3 17.0 %copy-start.5 = (f32[512,1024]{1,0:T(8,128)S(1)}, f32[512,1024]{1,0:T(8,128)}, u32[]{:S(2)}) copy-start(f32[512,1024]{1,0:T(8,128)} %convolution_bitcast_fusion) | copy-start | bytes 6291460
  219.8 668.0 %copy-start.125 = (f32[512]{0:T(512)S(1)}, f32[512]{0:T(512)}, u32[]{:S(2)}) copy-start(f32[512]{0:T(512)} %param.19) | copy-start | bytes 6148
  219.8 668.0 %copy-start.126 = (f32[128]{0:T(128)S(1)}, f32[128]{0:T(128)}, u32[]{:S(2)}) copy-start(f32[128]{0:T(128)} %rsqrt.55) | copy-start | bytes 1540
  219.8 669.1 %copy-start.11 = (f32[128,512]{1,0:T(8,128)S(1)}, f32[128,512]{1,0:T(8,128)}, u32[]{:S(2)}) copy-start(f32[128,512]{1,0:T(8,128)} %copy-done.10) | copy-start | bytes 786436
  219.8 670.9 %copy-start.1 = (bf16[1024,512]{1,0:T(8,128)(2,1)S(1)}, bf16[1024,512]{1,0:T(8,128)(2,1)}, u32[]{:S(2)}) copy-start(bf16[1024,512]{1,0:T(8,128)(2,1)} %param.24) | copy-start | bytes 3145732
  (76 other events, 250.0 us)
Sparse Core Ops, SparseCore 0:
  50.2 41.0 all-reduce.36
  102.6 34.0 all-reduce.38
  813.1 74.6 all-reduce.40
where the time goes:
time: 903 us; the launch traced here: 897 us
  blocking collectives  593 us (66%)
  waiting for transfers between devices  139 us (15%)
  local copies, waits for them, and re-layouts  46.2 us (5%)
  matrix products  45 us (5%)
  other arithmetic  34.5 us (4%)
  starting transfers between devices  22.7 us (3%)
  between operations  17.2 us (2%)
    unnamed x1, blocking collectives  593 us
    psum x3, waiting for transfers between devices, channel_total(): lax.psum(partial_value.astype(jnp.bfloat16), 'ch').astype(jnp.float32)  130 us
  transfers between devices with their start and end apart: 11, of which 7 were waited for; matrix products, arithmetic and copies ran while one was open for 3% of the time, Pallas kernels for 0%

commit v1 on v0

v1 whole, which is shorter than its diff:
```python
import jax
import jax.numpy as jnp
from jax import lax
from jax.experimental import pallas as pl
from jax.experimental.pallas import tpu as pltpu
from jax.sharding import PartitionSpec as P

HEADS = 8
RADIUS = 7
EPS = 1e-06
MESH = pl.DeviceIdType.MESH
F32 = jnp.float32
BF16 = jnp.bfloat16

TOK = 128
HALF = 64
KEYS = 768
WIDTH = 512
INNER = 256
HID = 1024
NROW, NCOL = 8, 16
NX, NZ = 4, 8


def nn(a, b):
    return lax.dot_general(a, b, (((1,), (0,)), ((), ())), preferred_element_type=F32)


def nt(a, b):
    return lax.dot_general(a, b, (((1,), (1,)), ((), ())), preferred_element_type=F32)


def tn(a, b):
    return lax.dot_general(a, b, (((0,), (0,)), ((), ())), preferred_element_type=F32)


def erf(x):
    return lax.erf(x)


def norm_scale(v):
    return lax.rsqrt(jnp.mean(v * v, axis=-1, keepdims=True) + EPS)


def norm_back(v, gain, upstream):
    s = norm_scale(v)
    n = v * s
    e = upstream * gain
    return s * (e - n * jnp.mean(e * n, axis=-1, keepdims=True))


def to_halves(block):
    return jnp.concatenate(
        [block[:, :8].reshape(HALF, WIDTH), block[:, 8:].reshape(HALF, WIDTH)], axis=0
    )


def from_halves(flat):
    return jnp.concatenate(
        [flat[:HALF].reshape(8, 8, WIDTH), flat[HALF:].reshape(8, 8, WIDTH)], axis=1
    )


class Links:
    def __init__(self, send, recv):
        self.send, self.recv, self.count, self.open = send, recv, 0, []

    def start(self, src, dst, device):
        copy = pltpu.make_async_remote_copy(
            src_ref=src,
            dst_ref=dst,
            send_sem=self.send.at[self.count],
            recv_sem=self.recv.at[self.count],
            device_id=device,
            device_id_type=MESH,
        )
        self.count += 1
        copy.start()
        self.open.append(copy)
        return copy

    def finish(self):
        for copy in self.open:
            copy.wait_send()


class Piece:
    def __init__(self, links, place, refs, out):
        self.links, self.place, self.out = links, place, out
        self.part, self.rc, self.xs, self.rx, self.ys, self.ry, self.zs, self.rz, self.fs = refs

    def core(self):
        core = self.place["core"]
        self.copy = self.links.start(
            self.part.at[1 - core], self.rc, self.place["core_peer"]
        )

    def x(self):
        p = self.place
        self.copy.wait_recv()
        for i in range(NX):
            rows = pl.ds(i * 128, 128)
            mine = self.part[p["core"], rows, :].astype(F32)
            self.xs[i] = (mine + self.rc[rows, :].astype(F32)).astype(BF16)
        self.copies = [
            self.links.start(
                self.xs.at[lax.rem(p["x"] + d, NX)], self.rx.at[d - 1], p["x_peer"][d]
            )
            for d in range(1, NX)
        ]

    def y(self):
        p = self.place
        for copy in self.copies:
            copy.wait_recv()
        total = self.xs[p["x"]].astype(F32)
        for d in range(NX - 1):
            total = total + self.rx[d].astype(F32)
        total = total.astype(BF16)
        self.ys[0] = total[:64]
        self.ys[1] = total[64:]
        self.copy = self.links.start(self.ys.at[1 - p["y"]], self.ry, p["y_peer"])

    def z(self):
        p = self.place
        self.copy.wait_recv()
        total = (self.ys[p["y"]].astype(F32) + self.ry[...].astype(F32)).astype(BF16)
        wide = total.shape[1] // 2
        for low in range(2):
            for high in range(4):
                self.zs[2 * high + low] = total[
                    16 * high : 16 * high + 16, low * wide : (low + 1) * wide
                ]
        self.copies = [
            self.links.start(
                self.zs.at[lax.rem(p["z"] + d, NZ)], self.rz.at[d - 1], p["z_peer"][d]
            )
            for d in range(1, NZ)
        ]

    def regather(self):
        p = self.place
        for copy in self.copies:
            copy.wait_recv()
        total = self.zs[p["z"]].astype(F32)
        for d in range(NZ - 1):
            total = total + self.rz[d].astype(F32)
        slot = 2 * p["core"] + p["z_low"]
        self.fs[slot] = total.astype(BF16)
        self.copies = [
            self.links.start(self.fs.at[slot], self.fs.at[slot], device)
            for device in p["near_peers"]
        ]

    def store(self):
        p = self.place
        for copy in self.copies:
            copy.wait_recv()
        for slot in range(4):
            rows = self.fs[slot].astype(F32)
            rows = jnp.where(p["z_low"] == 0, rows[:8], rows[8:])
            rows = jnp.where(p["core"] == 0, rows[:4], rows[4:])
            wide = rows.shape[1]
            self.out[:, slot * wide : (slot + 1) * wide] = rows.astype(BF16)


PIECES = (1024, 2048, 512, 512)


def piece_scratch(n):
    return [
        pltpu.VMEM((2, WIDTH, n // 2), BF16),
        pltpu.VMEM((WIDTH, n // 2), BF16),
        pltpu.VMEM((NX, 128, n // 2), BF16),
        pltpu.VMEM((NX - 1, 128, n // 2), BF16),
        pltpu.VMEM((2, 64, n // 2), BF16),
        pltpu.VMEM((64, n // 2), BF16),
        pltpu.VMEM((NZ, 16, n // 4), BF16),
        pltpu.VMEM((NZ - 1, 16, n // 4), BF16),
        pltpu.VMEM((4, 16, n // 4), BF16),
    ]


PER_PIECE = 9
MESSAGES = 96


def kernel(*refs):
    (tok, gout, attn_gain, mlp_gain, head_scale, wqkv_h, wout_h, wup_h, wdown_h) = refs[:9]
    (out_o, gin_o, gdown_o, gup_o, goq_o, gkv_o) = refs[9:15]
    refs = refs[15:]
    piece_refs = [refs[i * PER_PIECE : (i + 1) * PER_PIECE] for i in range(len(PIECES))]
    (
        wqkv,
        wout,
        wup,
        wdown,
        win,
        qmask,
        gmask,
        bias,
        probs,
        plow,
        dprob,
        dscore,
        raw,
        resid,
        gresid,
        ain,
        mlpin,
        fgrad,
        att,
        ghid,
        hidden,
        gmix,
        gproj,
        sums,
        sums_in,
        acc,
        rim_out,
        rim_in,
        ver_out,
        ver_in,
        send_sem,
        recv_sem,
        local_sem,
    ) = refs[len(PIECES) * PER_PIECE :]

    row, col, ch = lax.axis_index("row"), lax.axis_index("col"), lax.axis_index("ch")
    x, y = row // 2, lax.rem(row, 2)
    z, core = col // 2, lax.rem(col, 2)
    z_low = lax.rem(z, 2)
    above = (lax.rem(row + NROW - 1, NROW), col, ch)
    below = (lax.rem(row + 1, NROW), col, ch)
    left = (row, lax.rem(col + NCOL - 1, NCOL), ch)
    right = (row, lax.rem(col + 1, NCOL), ch)
    twin = (row, col, 1 - ch)
    z_flip = z + 1 - 2 * z_low
    x_peer = [(lax.rem(x + d, NX) * 2 + y, col, ch) for d in range(NX)]
    z_peer = [(row, lax.rem(z + d, NZ) * 2 + core, ch) for d in range(NZ)]
    core_peer = (row, z * 2 + 1 - core, ch)
    across = (row, z_flip * 2 + 1 - core, ch)
    place = {
        "x": x,
        "y": y,
        "z": z,
        "core": core,
        "z_low": z_low,
        "core_peer": core_peer,
        "y_peer": (x * 2 + 1 - y, col, ch),
        "x_peer": x_peer,
        "z_peer": z_peer,
        "near_peers": [core_peer, (row, z_flip * 2 + core, ch), across],
    }
    links = Links(send_sem, recv_sem)
    outs = (gdown_o, gup_o, goq_o, gkv_o)
    down_p, up_p, oq_p, kv_p = [
        Piece(links, place, r, o) for r, o in zip(piece_refs, outs)
    ]

    loads = []
    for i, (src, dst) in enumerate(
        ((wqkv_h, wqkv), (wdown_h, wdown), (wout_h, wout), (wup_h, wup))
    ):
        load = pltpu.make_async_copy(src, dst, local_sem.at[i])
        load.start()
        loads.append(load)

    barrier = pltpu.get_barrier_semaphore()
    peers = [above, below, left, right, twin, across] + x_peer[1:] + z_peer[1:]
    for peer in peers:
        pl.semaphore_signal(barrier, inc=1, device_id=peer, device_id_type=MESH)

    lane = lax.broadcasted_iota(jnp.int32, (1, INNER), 1) // 64
    same_head = (
        lax.broadcasted_iota(jnp.int32, (INNER, INNER), 0) // 64
        == lax.broadcasted_iota(jnp.int32, (INNER, INNER), 1) // 64
    )
    ones = jnp.where(same_head, 1.0, 0.0).astype(BF16)

    def head_sum(values):
        high = values.astype(BF16)
        low = (values - high.astype(F32)).astype(BF16)
        return nn(high, ones) + nn(low, ones)

    def head_rows(values):
        return [jnp.where(lane == h, values, jnp.zeros_like(values)) for h in range(4)]

    scale = jnp.zeros((1, INNER), F32)
    for h in range(4):
        scale = jnp.where(lane == h, head_scale[h], scale)

    toks = to_halves(tok[...].astype(F32))
    a = (toks * norm_scale(toks) * attn_gain[...]).astype(BF16)
    ain[...] = a
    fgrad[...] = to_halves(gout[...].astype(F32)).astype(BF16)
    loads[0].wait()
    key_raw = nn(a, wqkv[:, INNER : 2 * INNER])
    key_norm = lax.rsqrt(head_sum(key_raw * key_raw) + EPS)
    keys = (key_raw * key_norm).astype(BF16)
    win[0, 1, 1] = keys[:HALF]
    win[0, 2, 1] = keys[HALF:]
    raw[2] = key_raw
    raw[3] = key_norm
    pl.semaphore_wait(barrier, len(peers))

    def vertical(kv):
        return [
            links.start(win.at[kv, pl.ds(1, 2), 1], win.at[kv, pl.ds(1, 2), 0], below),
            links.start(win.at[kv, pl.ds(1, 2), 1], win.at[kv, pl.ds(1, 2), 2], above),
        ]

    def horizontal(kv, i):
        return [
            links.start(win.at[kv, 2, i], win.at[kv, 0, i], right),
            links.start(win.at[kv, 1, i], win.at[kv, 3, i], left),
        ]

    key_vert = vertical(0)
    key_side = horizontal(0, 1)
    values = nn(a, wqkv[:, 2 * INNER :]).astype(BF16)
    win[1, 1, 1] = values[:HALF]
    win[1, 2, 1] = values[HALF:]
    value_vert = vertical(1)
    value_side = horizontal(1, 1)

    query_raw = nn(a, wqkv[:, :INNER])
    query_norm = lax.rsqrt(head_sum(query_raw * query_raw) + EPS)
    raw[0] = query_raw
    raw[1] = query_norm
    queries = (query_raw * query_norm * scale).astype(BF16)
    for h, part in enumerate(head_rows(queries)):
        qmask[h * TOK : (h + 1) * TOK, :] = part

    def bias_rows(i, carry):
        t = lax.broadcasted_iota(jnp.int32, (32, KEYS), 0) + i * 32
        k = lax.broadcasted_iota(jnp.int32, (32, KEYS), 1)
        j = (
            jnp.where(k >= 192, 1, 0) + jnp.where(k >= 384, 1, 0) + jnp.where(k >= 576, 1, 0)
        )
        in_strip = k - 192 * j
        key_row = (in_strip >> 3) - 8
        key_col = (j - 1) * 8 + (k & 7)
        query_row = (t & 63) >> 3
        query_col = (t >> 6) * 8 + (t & 7)
        down, across_by = key_row - query_row, key_col - query_col
        at_row, at_col = row * 8 + key_row, col * 16 + key_col
        ok = (down >= -RADIUS) & (down <= RADIUS)
        ok = ok & (across_by >= -RADIUS) & (across_by <= RADIUS)
        ok = ok & (at_row >= 0) & (at_row < 8 * NROW) & (at_col >= 0) & (at_col < 16 * NCOL)
        bias[pl.ds(pl.multiple_of(i * 32, 32), 32), :] = jnp.where(ok, 0.0, -1e30)
        return carry

    lax.fori_loop(0, 4, bias_rows, 0)

    loads[1].wait()
    ghid[...] = nt(fgrad[...], wdown[...])

    for copy in key_vert:
        copy.wait_recv()
    key_side += horizontal(0, 0) + horizontal(0, 2)
    for copy in value_vert:
        copy.wait_recv()
    value_side += horizontal(1, 0) + horizontal(1, 2)
    for copy in key_side:
        copy.wait_recv()

    key_window = win[0].reshape(KEYS, INNER)
    probs[...] = nt(qmask[...], key_window)

    def softmax_rows(i, carry):
        rows = pl.ds(pl.multiple_of(i * 32, 32), 32)
        s = probs[rows, :] + bias[pl.ds(pl.multiple_of((i % 4) * 32, 32), 32), :]
        e = jnp.exp(s - jnp.max(s, axis=-1, keepdims=True))
        p = e * (1.0 / jnp.sum(e, axis=-1, keepdims=True))
        probs[rows, :] = p
        plow[rows, :] = p.astype(BF16)
        return carry

    lax.fori_loop(0, 16, softmax_rows, 0)
    for copy in value_side:
        copy.wait_recv()
    value_window = win[1].reshape(KEYS, INNER)

    def fold_heads(stacked):
        total = jnp.where(lane == 0, stacked[:TOK], 0.0)
        for h in range(1, 4):
            total = total + jnp.where(lane == h, stacked[h * TOK : (h + 1) * TOK], 0.0)
        return total

    attended = fold_heads(nn(plow[...], value_window)).astype(BF16)
    att[...] = attended
    loads[2].wait()

    def exchange(slot, value):
        sums[slot] = value.astype(BF16)
        return links.start(sums.at[slot], sums_in.at[slot], twin)

    def total_of(slot, copy):
        copy.wait_recv()
        return sums[slot].astype(F32) + sums_in[slot].astype(F32)

    attn_sum = exchange(0, nn(attended, wout[...]))
    loads[3].wait()
    residual = to_halves(tok[...].astype(F32)) + total_of(0, attn_sum)
    resid[...] = residual
    m = (residual * norm_scale(residual) * mlp_gain[...]).astype(BF16)
    mlpin[...] = m

    for j in range(4):
        cols = slice(j * 256, (j + 1) * 256)
        cols_v = slice(HID + j * 256, HID + (j + 1) * 256)
        gate = nn(m, wup[:, cols])
        val = nn(m, wup[:, cols_v])
        cdf = 0.5 * (1.0 + erf(gate * 0.7071067811865476))
        density = jnp.exp(-0.5 * gate * gate) * 0.3989422804014327
        act = gate * cdf
        hidden[:, cols] = (act * val).astype(BF16)
        gh = ghid[:, cols]
        gmix[:, cols] = (gh * val * (cdf + gate * density)).astype(BF16)
        gmix[:, cols_v] = (gh * act).astype(BF16)
    mlp_back = exchange(1, nt(gmix[...], wup[...]))
    mlp_sum = exchange(2, nn(hidden[...], wdown[...]))

    down_p.part[0] = tn(fgrad[...], hidden[:, :512]).astype(BF16)
    down_p.part[1] = tn(fgrad[...], hidden[:, 512:]).astype(BF16)
    down_p.core()
    up_p.part[0] = tn(mlpin[...], gmix[:, :HID]).astype(BF16)
    up_p.part[1] = tn(mlpin[...], gmix[:, HID:]).astype(BF16)
    up_p.core()
    down_p.x()

    grad_resid = to_halves(gout[...].astype(F32)) + norm_back(
        resid[...], mlp_gain[...], total_of(1, mlp_back)
    )
    gresid[...] = grad_resid
    grad_low = grad_resid.astype(BF16)
    grad_att = nt(grad_low, wout[...]).astype(BF16)
    for h, part in enumerate(head_rows(grad_att)):
        gmask[h * TOK : (h + 1) * TOK, :] = part

    def rims(kv, whole):
        whole = whole.reshape(4, 3, HALF, INNER)
        acc[kv] = whole[1:3]
        rim_out[kv, 0] = whole[0].astype(BF16)
        rim_out[kv, 1] = whole[3].astype(BF16)
        return [
            links.start(rim_out.at[kv, 0], rim_in.at[kv, 0], left),
            links.start(rim_out.at[kv, 1], rim_in.at[kv, 1], right),
        ]

    value_rims = rims(1, tn(plow[...], gmask[...]))
    dprob[...] = nt(gmask[...], win[1].reshape(KEYS, INNER))

    def score_rows(i, carry):
        rows = pl.ds(pl.multiple_of(i * 32, 32), 32)
        p, g = probs[rows, :], dprob[rows, :]
        delta = jnp.sum(p * g, axis=-1, keepdims=True)
        dscore[rows, :] = (p * (g - delta)).astype(BF16)
        return carry

    lax.fori_loop(0, 16, score_rows, 0)
    key_rims = rims(0, tn(dscore[...], qmask[...]))

    def through_norm(which, incoming, factor):
        v, r = raw[2 * which], raw[2 * which + 1]
        along = head_sum(v * incoming)
        return factor * r * (incoming - r * r * v * along)

    grad_query = fold_heads(nn(dscore[...], win[0].reshape(KEYS, INNER)))
    gproj[:, :INNER] = through_norm(0, grad_query, scale).astype(BF16)
    oq_p.part[0] = tn(gresid[...].astype(BF16), att[...]).astype(BF16)
    oq_p.part[1] = tn(ain[...], gproj[:, :INNER]).astype(BF16)
    oq_p.core()

    def turn(kv, copies):
        for copy in copies:
            copy.wait_recv()
        acc[kv, 1] = acc[kv, 1] + rim_in[kv, 0].astype(F32)
        acc[kv, 0] = acc[kv, 0] + rim_in[kv, 1].astype(F32)
        ver_out[kv, 0] = acc[kv, :, 0].astype(BF16)
        ver_out[kv, 1] = acc[kv, :, 2].astype(BF16)
        return [
            links.start(ver_out.at[kv, 0], ver_in.at[kv, 0], above),
            links.start(ver_out.at[kv, 1], ver_in.at[kv, 1], below),
        ]

    value_turn = turn(1, value_rims)
    key_turn = turn(0, key_rims)
    up_p.x()
    out_o[...] = from_halves(resid[...] + total_of(2, mlp_sum)).astype(BF16)
    oq_p.x()
    down_p.y()

    def owned(kv, copies):
        for copy in copies:
            copy.wait_recv()
        mine = acc[kv, :, 1] + ver_in[kv, 0].astype(F32) + ver_in[kv, 1].astype(F32)
        return mine.reshape(TOK, INNER)

    gproj[:, 2 * INNER :] = owned(1, value_turn).astype(BF16)
    gproj[:, INNER : 2 * INNER] = through_norm(1, owned(0, key_turn), 1.0).astype(BF16)
    in_back = exchange(3, nt(gproj[...], wqkv[...]))
    kv_p.part[0] = tn(ain[...], gproj[:, INNER : 2 * INNER]).astype(BF16)
    kv_p.part[1] = tn(ain[...], gproj[:, 2 * INNER :]).astype(BF16)
    kv_p.core()
    up_p.y()
    oq_p.y()
    down_p.z()
    kv_p.x()
    grad_in = gresid[...] + norm_back(
        to_halves(tok[...].astype(F32)), attn_gain[...], total_of(3, in_back)
    )
    gin_o[...] = from_halves(grad_in).astype(BF16)
    up_p.z()
    oq_p.z()
    kv_p.y()
    down_p.regather()
    up_p.regather()
    kv_p.z()
    oq_p.regather()
    kv_p.regather()
    down_p.store()
    up_p.store()
    oq_p.store()
    kv_p.store()
    links.finish()


def shards(tokens, grad_output, attn_gain, mlp_gain, w_qkv, w_out, w_up, w_down, head_scale):
    rows, cols, width = tokens.shape
    vmem = pl.BlockSpec(memory_space=pltpu.VMEM)
    anywhere = pl.BlockSpec(memory_space=pl.ANY)
    out_shape = [
        jax.ShapeDtypeStruct(tokens.shape, BF16),
        jax.ShapeDtypeStruct(tokens.shape, BF16),
    ] + [jax.ShapeDtypeStruct((4, n), BF16) for n in PIECES]
    scratch = []
    for n in PIECES:
        scratch += piece_scratch(n)
    scratch += [
        pltpu.VMEM((WIDTH, 3 * INNER), BF16),
        pltpu.VMEM((INNER, WIDTH), BF16),
        pltpu.VMEM((WIDTH, 2 * HID), BF16),
        pltpu.VMEM((HID, WIDTH), BF16),
        pltpu.VMEM((2, 4, 3, HALF, INNER), BF16),
        pltpu.VMEM((4 * TOK, INNER), BF16),
        pltpu.VMEM((4 * TOK, INNER), BF16),
        pltpu.VMEM((TOK, KEYS), F32),
        pltpu.VMEM((4 * TOK, KEYS), F32),
        pltpu.VMEM((4 * TOK, KEYS), BF16),
        pltpu.VMEM((4 * TOK, KEYS), F32),
        pltpu.VMEM((4 * TOK, KEYS), BF16),
        pltpu.VMEM((4, TOK, INNER), F32),
        pltpu.VMEM((TOK, WIDTH), F32),
        pltpu.VMEM((TOK, WIDTH), F32),
        pltpu.VMEM((TOK, WIDTH), BF16),
        pltpu.VMEM((TOK, WIDTH), BF16),
        pltpu.VMEM((TOK, WIDTH), BF16),
        pltpu.VMEM((TOK, INNER), BF16),
        pltpu.VMEM((TOK, HID), F32),
        pltpu.VMEM((TOK, HID), BF16),
        pltpu.VMEM((TOK, 2 * HID), BF16),
        pltpu.VMEM((TOK, 3 * INNER), BF16),
        pltpu.VMEM((4, TOK, WIDTH), BF16),
        pltpu.VMEM((4, TOK, WIDTH), BF16),
        pltpu.VMEM((2, 2, 3, HALF, INNER), F32),
        pltpu.VMEM((2, 2, 3, HALF, INNER), BF16),
        pltpu.VMEM((2, 2, 3, HALF, INNER), BF16),
        pltpu.VMEM((2, 2, 2, HALF, INNER), BF16),
        pltpu.VMEM((2, 2, 2, HALF, INNER), BF16),
        pltpu.SemaphoreType.DMA((MESSAGES,)),
        pltpu.SemaphoreType.DMA((MESSAGES,)),
        pltpu.SemaphoreType.DMA((4,)),
    ]
    out, grad_input, gdown, gup, goq, gkv = pl.pallas_call(
        kernel,
        out_shape=out_shape,
        in_specs=[vmem] * 4
        + [pl.BlockSpec(memory_space=pltpu.SMEM)]
        + [anywhere] * 4,
        out_specs=[vmem] * 6,
        scratch_shapes=scratch,
        compiler_params=pltpu.CompilerParams(
            collective_id=0, has_side_effects=True, vmem_limit_bytes=58 * 1024 * 1024
        ),
    )(
        tokens,
        grad_output,
        attn_gain.reshape(1, width),
        mlp_gain.reshape(1, width),
        head_scale,
        w_qkv.reshape(width, 3 * INNER),
        w_out,
        w_up.reshape(width, 2 * HID),
        w_down,
    )
    grad_qkv = jnp.concatenate([goq[:, INNER:], gkv], axis=1).reshape(4, 3, INNER)
    return out, grad_input, grad_qkv, goq[:, :INNER], gup.reshape(4, 2, HID), gdown


def solution(mesh):
    placed = (
        P("row", "col", None),
        P("row", "col", None),
        P(),
        P(),
        P(None, None, "ch"),
        P("ch", None),
        P(None, None, "ch"),
        P("ch", None),
        P("ch"),
    )
    return jax.shard_map(
        shards,
        mesh=mesh,
        in_specs=placed,
        out_specs=(
            P("row", "col", None),
            P("row", "col", None),
            P(("row", "col"), None, "ch"),
            P(("row", "col"), "ch"),
            P(("row", "col"), None, "ch"),
            P(("row", "col"), "ch"),
        ),
        check_vma=False,
    )
```

time: 903 us -> 93.6 us (0.10)
  the two profiles are of different devices: /device:TPU:8 before, /device:TPU:1 now
where the time goes in v1:
time: 93.6 us; the launch traced here: 93.3 us
  Pallas kernels  79.6 us (85%)
  local copies, waits for them, and re-layouts  11.7 us (12%)
  other arithmetic  1.28 us (1%)
    pallas_call x1, Pallas kernels, shards(): pl.pallas_call(kernel, out_shape=out_shape, in_specs=[vmem] * 4 + [pl.Blo...  79.6 us
    unnamed x7, local copies, waits for them, and re-layouts  7.95 us

profile of v1, /device:TPU:1, one launch (start us, length us, event | category | flops | bytes accessed | tf_op | source)
XLA Modules:
  0.0 93.3 jit_solution(11545147876905184527)
XLA Ops:
  0.6 0.0 copy-start
  0.6 1.6 %copy.17 = bf16[512,3,256]{0,2,1:T(8,128)(2,1)S(1)} copy(bf16[512,3,256]{2,0,1:T(8,128)(2,1)} %param.13) | data formatting | bytes 1572864 | tf_op args[4]
  2.2 1.2 %copy.18.refs_5_ = bf16[512,768]{1,0:T(8,128)(2,1)} copy(bf16[512,768]{0,1:T(8,128)(2,1)S(1)} %bitcast.7) | data formatting | bytes 1572864 | tf_op jit(solution)/shard_map/reshape | solution.py:593
  3.4 0.0 copy-done
  3.4 1.9 %copy.19 = bf16[64,8,2,1024]{3,1,2,0:T(8,128)(2,1)} copy(bf16[64,8,2,1024]{3,2,1,0:T(2,128)(2,1)S(1)} %bitcast.8) | data formatting | bytes 4194304
  5.3 79.6 %shard_map.136 = (bf16[8,16,512]{2,1,0:T(8,128)(2,1)}, bf16[8,16,512]{2,1,0:T(8,128)(2,1)}, bf16[4,1024]{1,0:T(4,128)(2,1)}, bf16[4,2048]{1,0:T(4,128)(2,1)}, bf...) custom-call(bf16[8,16,512]{2,1,0:T(8,128)(2,1)} %refs_0_.1, bf16[8,16,512]{2,1,0:T(8,128)(2,1)} %refs_1_.1, ...), custom_call_target="tpu_custom_call" | custom-call | tf_op jit(solution)/shard_map/pallas_call | solution.py:576
  85.0 1.2 %fusion = (bf16[4,256]{1,0:T(4,128)(2,1)}, bf16[4,256]{1,0:T(4,128)(2,1)S(1)}) fusion(bf16[4,512]{1,0:T(4,128)(2,1)} %get-tuple-element.14), kind=kLoop, calls=%fused_computation.1 | loop fusion | bytes 8192 | tf_op jit(solution)/shard_map/slice | solution.py:599
  86.2 1.3 %pad_maximum_fusion = bf16[4,768]{1,0:T(4,128)(2,1)} fusion(bf16[4,512]{1,0:T(4,128)(2,1)} %get-tuple-element.15, bf16[4,256]{1,0:T(4,128)(2,1)S(1)} %get-tuple-element.25), kind=kLoop, calls=%fused_computation | loop fusion | flops 12288 | bytes 12288 | tf_op jit(solution)/shard_map/concatenate | solution.py:598
  87.5 1.3 %reshape.35 = bf16[4,2,1024]{2,1,0:T(2,128)(2,1)} reshape(bf16[4,2048]{1,0:T(4,128)(2,1)} %get-tuple-element.16) | data formatting | bytes 32768 | tf_op jit(solution)/shard_map/reshape | solution.py:599
  88.8 1.6 %copy.23 = bf16[8,16,512]{2,1,0:T(8,128)(2,1)} copy(bf16[8,16,512]{2,1,0:T(8,128)(2,1)} %get-tuple-element.32) | data formatting | bytes 262144
  90.4 1.6 %copy.24 = bf16[8,16,512]{2,1,0:T(8,128)(2,1)} copy(bf16[8,16,512]{2,1,0:T(8,128)(2,1)} %get-tuple-element.33) | data formatting | bytes 262144
  92.0 1.3 %copy.25 = bf16[4,1024]{1,0:T(4,128)(2,1)} copy(bf16[4,1024]{1,0:T(4,128)(2,1)} %get-tuple-element.37) | data formatting | bytes 16384
Async XLA Ops:
  0.6 2.8 %copy-start = (bf16[512,2,1024]{2,1,0:T(2,128)(2,1)S(1)}, bf16[512,2,1024]{2,1,0:T(2,128)(2,1)}, u32[]{:S(2)}) copy-start(bf16[512,2,1024]{2,1,0:T(2,128)(2,1)} %param.15) | copy-start | bytes 6291460

commit v2 on v1

--- a/solution.py
+++ b/solution.py
@@ -87,7 +87,13 @@
 class Piece:
     def __init__(self, links, place, refs, out):
         self.links, self.place, self.out = links, place, out
-        self.part, self.rc, self.xs, self.rx, self.ys, self.ry, self.zs, self.rz, self.fs = refs
+        self.part, self.rc, self.xs, self.r1, self.s2, self.r2, self.ys, self.ry, self.zs, self.rz = refs
+
+    def fill(self, left_t, right, at=0):
+        wide = right.shape[1]
+        for c in range(2):
+            product = nn(left_t[c * 256 : (c + 1) * 256, :], right)
+            self.part[c, :, at : at + wide] = product.astype(BF16)
 
     def core(self):
         core = self.place["core"]
@@ -95,42 +101,66 @@
             self.part.at[1 - core], self.rc, self.place["core_peer"]
         )
 
-    def x(self):
+    def x1(self):
         p = self.place
         self.copy.wait_recv()
+        wide = self.part.shape[2] // 2
         for i in range(NX):
-            rows = pl.ds(i * 128, 128)
-            mine = self.part[p["core"], rows, :].astype(F32)
-            self.xs[i] = (mine + self.rc[rows, :].astype(F32)).astype(BF16)
+            rows = pl.ds(i * 64, 64)
+            total = self.part[p["core"], rows, :].astype(F32) + self.rc[rows, :].astype(F32)
+            total = total.astype(BF16)
+            self.xs[0, i] = total[:, :wide]
+            self.xs[1, i] = total[:, wide:]
+        far = NX - 1 - p["x"]
+        plan = (
+            (0, 0, p["x_flip"], p["x_flip_peer"]),
+            (1, 0, far, p["x_far_peer"]),
+            (0, 1, p["x_both"], p["x_flip_peer"]),
+            (1, 1, p["x_both"], p["x_far_peer"]),
+        )
         self.copies = [
-            self.links.start(
-                self.xs.at[lax.rem(p["x"] + d, NX)], self.rx.at[d - 1], p["x_peer"][d]
-            )
-            for d in range(1, NX)
+            self.links.start(self.xs.at[side, block], self.r1.at[side, order], peer)
+            for side, order, block, peer in plan
         ]
+
+    def x2(self):
+        p = self.place
+        for copy in self.copies:
+            copy.wait_recv()
+        far = NX - 1 - p["x"]
+        self.copies = []
+        for side, block, peer in ((0, far, p["x_far_peer"]), (1, p["x_flip"], p["x_flip_peer"])):
+            total = self.xs[side, block].astype(F32) + self.r1[side, 1].astype(F32)
+            self.s2[side] = total.astype(BF16)
+            self.copies.append(self.links.start(self.s2.at[side], self.r2.at[side], peer))
 
     def y(self):
         p = self.place
         for copy in self.copies:
             copy.wait_recv()
-        total = self.xs[p["x"]].astype(F32)
-        for d in range(NX - 1):
-            total = total + self.rx[d].astype(F32)
-        total = total.astype(BF16)
-        self.ys[0] = total[:64]
-        self.ys[1] = total[64:]
+        wide = self.part.shape[2] // 2
+        for side in range(2):
+            total = self.xs[side, p["x"]].astype(F32) + self.r1[side, 0].astype(F32)
+            total = (total + self.r2[side].astype(F32)).astype(BF16)
+            for half in range(2):
+                self.ys[half, :, side * wide : (side + 1) * wide] = total[
+                    half * 32 : half * 32 + 32
+                ]
         self.copy = self.links.start(self.ys.at[1 - p["y"]], self.ry, p["y_peer"])
 
     def z(self):
+        self.copy.wait_recv()
+        self.z_of(self.ys[self.place["y"]].astype(F32) + self.ry[...].astype(F32))
+
+    def z_of(self, total):
         p = self.place
-        self.copy.wait_recv()
-        total = (self.ys[p["y"]].astype(F32) + self.ry[...].astype(F32)).astype(BF16)
-        wide = total.shape[1] // 2
-        for low in range(2):
-            for high in range(4):
-                self.zs[2 * high + low] = total[
-                    16 * high : 16 * high + 16, low * wide : (low + 1) * wide
-                ]
+        wide = total.shape[1] // 4
+        for k in range(NZ):
+            rows = total[4 * k : 4 * k + 4]
+            block = jnp.concatenate(
+                [rows[:, q * wide : (q + 1) * wide] for q in range(4)], axis=0
+            )
+            self.zs[k] = block.astype(BF16)
         self.copies = [
             self.links.start(
                 self.zs.at[lax.rem(p["z"] + d, NZ)], self.rz.at[d - 1], p["z_peer"][d]
@@ -138,30 +168,44 @@
             for d in range(1, NZ)
         ]
 
-    def regather(self):
+    def store(self):
         p = self.place
         for copy in self.copies:
             copy.wait_recv()
         total = self.zs[p["z"]].astype(F32)
         for d in range(NZ - 1):
             total = total + self.rz[d].astype(F32)
-        slot = 2 * p["core"] + p["z_low"]
-        self.fs[slot] = total.astype(BF16)
+        wide = total.shape[1]
+        for q in range(4):
+            self.out[:, q * wide : (q + 1) * wide] = total[4 * q : 4 * q + 4].astype(BF16)
+
+
+class LastPiece(Piece):
+    def __init__(self, links, place, refs, out):
+        self.links, self.place, self.out = links, place, out
+        self.part, self.rc, self.xs, self.r1, self.zs, self.rz = refs
+
+    def rows(self):
+        p = self.place
+        self.copy.wait_recv()
+        for i in range(NROW):
+            rows = pl.ds(i * 32, 32)
+            total = self.part[p["core"], rows, :].astype(F32) + self.rc[rows, :].astype(F32)
+            self.xs[i] = total.astype(BF16)
         self.copies = [
-            self.links.start(self.fs.at[slot], self.fs.at[slot], device)
-            for device in p["near_peers"]
+            self.links.start(
+                self.xs.at[lax.rem(p["row"] + d, NROW)], self.r1.at[d - 1], p["row_peer"][d]
+            )
+            for d in range(1, NROW)
         ]
 
-    def store(self):
-        p = self.place
+    def z(self):
         for copy in self.copies:
             copy.wait_recv()
-        for slot in range(4):
-            rows = self.fs[slot].astype(F32)
-            rows = jnp.where(p["z_low"] == 0, rows[:8], rows[8:])
-            rows = jnp.where(p["core"] == 0, rows[:4], rows[4:])
-            wide = rows.shape[1]
-            self.out[:, slot * wide : (slot + 1) * wide] = rows.astype(BF16)
+        total = self.xs[self.place["row"]].astype(F32)
+        for d in range(NROW - 1):
+            total = total + self.r1[d].astype(F32)
+        self.z_of(total)
 
 
 PIECES = (1024, 2048, 512, 512)
@@ -169,19 +213,32 @@
 
 def piece_scratch(n):
     return [
-        pltpu.VMEM((2, WIDTH, n // 2), BF16),
-        pltpu.VMEM((WIDTH, n // 2), BF16),
-        pltpu.VMEM((NX, 128, n // 2), BF16),
-        pltpu.VMEM((NX - 1, 128, n // 2), BF16),
+        pltpu.VMEM((2, 256, n), BF16),
+        pltpu.VMEM((256, n), BF16),
+        pltpu.VMEM((2, NX, 64, n // 2), BF16),
+        pltpu.VMEM((2, 2, 64, n // 2), BF16),
         pltpu.VMEM((2, 64, n // 2), BF16),
-        pltpu.VMEM((64, n // 2), BF16),
+        pltpu.VMEM((2, 64, n // 2), BF16),
+        pltpu.VMEM((2, 32, n), BF16),
+        pltpu.VMEM((32, n), BF16),
         pltpu.VMEM((NZ, 16, n // 4), BF16),
         pltpu.VMEM((NZ - 1, 16, n // 4), BF16),
-        pltpu.VMEM((4, 16, n // 4), BF16),
     ]
 
 
-PER_PIECE = 9
+def last_scratch(n):
+    return [
+        pltpu.VMEM((2, 256, n), BF16),
+        pltpu.VMEM((256, n), BF16),
+        pltpu.VMEM((NROW, 32, n), BF16),
+        pltpu.VMEM((NROW - 1, 32, n), BF16),
+        pltpu.VMEM((NZ, 16, n // 4), BF16),
+        pltpu.VMEM((NZ - 1, 16, n // 4), BF16),
+    ]
+
+
+PER_PIECE = 10
+PER_LAST = 6
 MESSAGES = 96
 
 
@@ -189,11 +246,14 @@
     (tok, gout, attn_gain, mlp_gain, head_scale, wqkv_h, wout_h, wup_h, wdown_h) = refs[:9]
     (out_o, gin_o, gdown_o, gup_o, goq_o, gkv_o) = refs[9:15]
     refs = refs[15:]
-    piece_refs = [refs[i * PER_PIECE : (i + 1) * PER_PIECE] for i in range(len(PIECES))]
+    piece_refs = [refs[i * PER_PIECE : (i + 1) * PER_PIECE] for i in range(3)]
+    refs = refs[3 * PER_PIECE :]
+    last_refs = refs[:PER_LAST]
     (
         wqkv,
         wout,
         wup,
+        wup_pairs,
         wdown,
         win,
         qmask,
@@ -209,6 +269,8 @@
         ain,
         mlpin,
         fgrad,
+        order,
+        left_t,
         att,
         ghid,
         hidden,
@@ -224,50 +286,49 @@
         send_sem,
         recv_sem,
         local_sem,
-    ) = refs[len(PIECES) * PER_PIECE :]
+    ) = refs[PER_LAST:]
 
     row, col, ch = lax.axis_index("row"), lax.axis_index("col"), lax.axis_index("ch")
     x, y = row // 2, lax.rem(row, 2)
     z, core = col // 2, lax.rem(col, 2)
-    z_low = lax.rem(z, 2)
     above = (lax.rem(row + NROW - 1, NROW), col, ch)
     below = (lax.rem(row + 1, NROW), col, ch)
     left = (row, lax.rem(col + NCOL - 1, NCOL), ch)
     right = (row, lax.rem(col + 1, NCOL), ch)
     twin = (row, col, 1 - ch)
-    z_flip = z + 1 - 2 * z_low
-    x_peer = [(lax.rem(x + d, NX) * 2 + y, col, ch) for d in range(NX)]
+    x_flip = x + 1 - 2 * lax.rem(x, 2)
+    row_peer = [(lax.rem(row + d, NROW), col, ch) for d in range(NROW)]
     z_peer = [(row, lax.rem(z + d, NZ) * 2 + core, ch) for d in range(NZ)]
-    core_peer = (row, z * 2 + 1 - core, ch)
-    across = (row, z_flip * 2 + 1 - core, ch)
     place = {
+        "row": row,
         "x": x,
         "y": y,
         "z": z,
         "core": core,
-        "z_low": z_low,
-        "core_peer": core_peer,
+        "x_flip": x_flip,
+        "x_both": NX - 1 - x_flip,
+        "x_flip_peer": (x_flip * 2 + y, col, ch),
+        "x_far_peer": ((NX - 1 - x) * 2 + y, col, ch),
+        "core_peer": (row, z * 2 + 1 - core, ch),
         "y_peer": (x * 2 + 1 - y, col, ch),
-        "x_peer": x_peer,
+        "row_peer": row_peer,
         "z_peer": z_peer,
-        "near_peers": [core_peer, (row, z_flip * 2 + core, ch), across],
     }
     links = Links(send_sem, recv_sem)
-    outs = (gdown_o, gup_o, goq_o, gkv_o)
-    down_p, up_p, oq_p, kv_p = [
-        Piece(links, place, r, o) for r, o in zip(piece_refs, outs)
-    ]
+    outs = (gdown_o, gup_o, goq_o)
+    down_p, up_p, oq_p = [Piece(links, place, r, o) for r, o in zip(piece_refs, outs)]
+    kv_p = LastPiece(links, place, last_refs, gkv_o)
 
     loads = []
     for i, (src, dst) in enumerate(
-        ((wqkv_h, wqkv), (wdown_h, wdown), (wout_h, wout), (wup_h, wup))
+        ((wqkv_h, wqkv), (wdown_h, wdown), (wout_h, wout), (wup_h, wup_pairs))
     ):
         load = pltpu.make_async_copy(src, dst, local_sem.at[i])
         load.start()
         loads.append(load)
 
     barrier = pltpu.get_barrier_semaphore()
-    peers = [above, below, left, right, twin, across] + x_peer[1:] + z_peer[1:]
+    peers = [left, right, twin] + row_peer[1:] + z_peer[1:]
     for peer in peers:
         pl.semaphore_signal(barrier, inc=1, device_id=peer, device_id_type=MESH)
 
@@ -295,7 +356,7 @@
     ain[...] = a
     fgrad[...] = to_halves(gout[...].astype(F32)).astype(BF16)
     loads[0].wait()
-    key_raw = nn(a, wqkv[:, INNER : 2 * INNER])
+    key_raw = nn(a, wqkv[1])
     key_norm = lax.rsqrt(head_sum(key_raw * key_raw) + EPS)
     keys = (key_raw * key_norm).astype(BF16)
     win[0, 1, 1] = keys[:HALF]
@@ -318,13 +379,13 @@
 
     key_vert = vertical(0)
     key_side = horizontal(0, 1)
-    values = nn(a, wqkv[:, 2 * INNER :]).astype(BF16)
+    values = nn(a, wqkv[2]).astype(BF16)
     win[1, 1, 1] = values[:HALF]
     win[1, 2, 1] = values[HALF:]
     value_vert = vertical(1)
     value_side = horizontal(1, 1)
 
-    query_raw = nn(a, wqkv[:, :INNER])
+    query_raw = nn(a, wqkv[0])
     query_norm = lax.rsqrt(head_sum(query_raw * query_raw) + EPS)
     raw[0] = query_raw
     raw[1] = query_norm
@@ -353,7 +414,26 @@
 
     lax.fori_loop(0, 4, bias_rows, 0)
 
+    loads[3].wait()
+
+    def part_rows(i, carry):
+        rows = pl.ds(pl.multiple_of(i * 16, 16), 16)
+        both = wup_pairs[rows].astype(F32)
+        wup[rows, :HID] = both[:, 0, :].astype(BF16)
+        wup[rows, HID:] = both[:, 1, :].astype(BF16)
+        return carry
+
+    lax.fori_loop(0, WIDTH // 16, part_rows, 0)
+
+    at = lax.broadcasted_iota(jnp.int32, (WIDTH, WIDTH), 0)
+    of = lax.broadcasted_iota(jnp.int32, (WIDTH, WIDTH), 1)
+    to = ((of >> 2) & 1) * 256 + (of >> 3) * 4 + (of & 3)
+    order[...] = jnp.where(at == to, 1.0, 0.0).astype(BF16)
+    left_t[0] = nt(order[...], fgrad[...]).astype(BF16)
+    left_t[1] = nt(order[...], ain[...]).astype(BF16)
+
     loads[1].wait()
+    loads[2].wait()
     ghid[...] = nt(fgrad[...], wdown[...])
 
     for copy in key_vert:
@@ -390,7 +470,6 @@
 
     attended = fold_heads(nn(plow[...], value_window)).astype(BF16)
     att[...] = attended
-    loads[2].wait()
 
     def exchange(slot, value):
         sums[slot] = value.astype(BF16)
@@ -401,7 +480,6 @@
         return sums[slot].astype(F32) + sums_in[slot].astype(F32)
 
     attn_sum = exchange(0, nn(attended, wout[...]))
-    loads[3].wait()
     residual = to_halves(tok[...].astype(F32)) + total_of(0, attn_sum)
     resid[...] = residual
     m = (residual * norm_scale(residual) * mlp_gain[...]).astype(BF16)
@@ -422,13 +500,12 @@
     mlp_back = exchange(1, nt(gmix[...], wup[...]))
     mlp_sum = exchange(2, nn(hidden[...], wdown[...]))
 
-    down_p.part[0] = tn(fgrad[...], hidden[:, :512]).astype(BF16)
-    down_p.part[1] = tn(fgrad[...], hidden[:, 512:]).astype(BF16)
+    down_p.fill(left_t.at[0], hidden[...])
     down_p.core()
-    up_p.part[0] = tn(mlpin[...], gmix[:, :HID]).astype(BF16)
-    up_p.part[1] = tn(mlpin[...], gmix[:, HID:]).astype(BF16)
+    left_t[2] = nt(order[...], mlpin[...]).astype(BF16)
+    up_p.fill(left_t.at[2], gmix[...])
     up_p.core()
-    down_p.x()
+    down_p.x1()
 
     grad_resid = to_halves(gout[...].astype(F32)) + norm_back(
         resid[...], mlp_gain[...], total_of(1, mlp_back)
@@ -438,6 +515,8 @@
     grad_att = nt(grad_low, wout[...]).astype(BF16)
     for h, part in enumerate(head_rows(grad_att)):
         gmask[h * TOK : (h + 1) * TOK, :] = part
+
+    up_p.x1()
 
     def rims(kv, whole):
         whole = whole.reshape(4, 3, HALF, INNER)
@@ -450,6 +529,7 @@
         ]
 
     value_rims = rims(1, tn(plow[...], gmask[...]))
+    down_p.x2()
     dprob[...] = nt(gmask[...], win[1].reshape(KEYS, INNER))
 
     def score_rows(i, carry):
@@ -469,9 +549,11 @@
 
     grad_query = fold_heads(nn(dscore[...], win[0].reshape(KEYS, INNER)))
     gproj[:, :INNER] = through_norm(0, grad_query, scale).astype(BF16)
-    oq_p.part[0] = tn(gresid[...].astype(BF16), att[...]).astype(BF16)
-    oq_p.part[1] = tn(ain[...], gproj[:, :INNER]).astype(BF16)
+    left_t[3] = nt(order[...], gresid[...].astype(BF16)).astype(BF16)
+    oq_p.fill(left_t.at[3], att[...])
+    oq_p.fill(left_t.at[1], gproj[:, :INNER], INNER)
     oq_p.core()
+    up_p.x2()
 
     def turn(kv, copies):
         for copy in copies:
@@ -487,10 +569,9 @@
 
     value_turn = turn(1, value_rims)
     key_turn = turn(0, key_rims)
-    up_p.x()
+    down_p.y()
     out_o[...] = from_halves(resid[...] + total_of(2, mlp_sum)).astype(BF16)
-    oq_p.x()
-    down_p.y()
+    oq_p.x1()
 
     def owned(kv, copies):
         for copy in copies:
@@ -500,31 +581,41 @@
 
     gproj[:, 2 * INNER :] = owned(1, value_turn).astype(BF16)
     gproj[:, INNER : 2 * INNER] = through_norm(1, owned(0, key_turn), 1.0).astype(BF16)
-    in_back = exchange(3, nt(gproj[...], wqkv[...]))
-    kv_p.part[0] = tn(ain[...], gproj[:, INNER : 2 * INNER]).astype(BF16)
-    kv_p.part[1] = tn(ain[...], gproj[:, 2 * INNER :]).astype(BF16)
+    back = nt(gproj[:, :INNER], wqkv[0]) + nt(gproj[:, INNER : 2 * INNER], wqkv[1])
+    in_back = exchange(3, back + nt(gproj[:, 2 * INNER :], wqkv[2]))
+    kv_p.fill(left_t.at[1], gproj[:, INNER:])
     kv_p.core()
     up_p.y()
+    oq_p.x2()
+    down_p.z()
+    kv_p.rows()
     oq_p.y()
-    down_p.z()
-    kv_p.x()
     grad_in = gresid[...] + norm_back(
         to_halves(tok[...].astype(F32)), attn_gain[...], total_of(3, in_back)
     )
     gin_o[...] = from_halves(grad_in).astype(BF16)
     up_p.z()
     oq_p.z()
-    kv_p.y()
-    down_p.regather()
-    up_p.regather()
     kv_p.z()
-    oq_p.regather()
-    kv_p.regather()
     down_p.store()
     up_p.store()
     oq_p.store()
     kv_p.store()
     links.finish()
+
+
+def laid_out(out, gin, gdown, gup, goq, gkv, out_o, gin_o, gqkv_o, gout_o, gup_o, gdown_o):
+    out_o[...] = out[...]
+    gin_o[...] = gin[...]
+    gdown_o[...] = gdown[...]
+    gout_o[...] = goq[:, :INNER]
+    gqkv_o[0] = goq[:, INNER:]
+    gqkv_o[1] = gkv[:, :INNER]
+    gqkv_o[2] = gkv[:, INNER:]
+    both = gup[...].astype(F32)
+    for r in range(4):
+        pair = jnp.concatenate([both[r : r + 1, :HID], both[r : r + 1, HID:]], axis=0)
+        gup_o[r] = pair.astype(BF16)
 
 
 def shards(tokens, grad_output, attn_gain, mlp_gain, w_qkv, w_out, w_up, w_down, head_scale):
@@ -536,12 +627,14 @@
         jax.ShapeDtypeStruct(tokens.shape, BF16),
     ] + [jax.ShapeDtypeStruct((4, n), BF16) for n in PIECES]
     scratch = []
-    for n in PIECES:
+    for n in PIECES[:3]:
         scratch += piece_scratch(n)
+    scratch += last_scratch(PIECES[3])
     scratch += [
-        pltpu.VMEM((WIDTH, 3 * INNER), BF16),
+        pltpu.VMEM((3, WIDTH, INNER), BF16),
         pltpu.VMEM((INNER, WIDTH), BF16),
         pltpu.VMEM((WIDTH, 2 * HID), BF16),
+        pltpu.VMEM((WIDTH, 2, HID), BF16),
         pltpu.VMEM((HID, WIDTH), BF16),
         pltpu.VMEM((2, 4, 3, HALF, INNER), BF16),
         pltpu.VMEM((4 * TOK, INNER), BF16),
@@ -557,6 +650,8 @@
         pltpu.VMEM((TOK, WIDTH), BF16),
         pltpu.VMEM((TOK, WIDTH), BF16),
         pltpu.VMEM((TOK, WIDTH), BF16),
+        pltpu.VMEM((WIDTH, WIDTH), BF16),
+        pltpu.VMEM((4, WIDTH, TOK), BF16),
         pltpu.VMEM((TOK, INNER), BF16),
         pltpu.VMEM((TOK, HID), F32),
         pltpu.VMEM((TOK, HID), BF16),
@@ -590,13 +685,25 @@
         attn_gain.reshape(1, width),
         mlp_gain.reshape(1, width),
         head_scale,
-        w_qkv.reshape(width, 3 * INNER),
+        jnp.transpose(w_qkv, (1, 0, 2)),
         w_out,
-        w_up.reshape(width, 2 * HID),
+        w_up,
         w_down,
     )
-    grad_qkv = jnp.concatenate([goq[:, INNER:], gkv], axis=1).reshape(4, 3, INNER)
-    return out, grad_input, grad_qkv, goq[:, :INNER], gup.reshape(4, 2, HID), gdown
+    out, grad_input, grad_qkv, grad_out_t, grad_up, grad_down_t = pl.pallas_call(
+        laid_out,
+        out_shape=[
+            jax.ShapeDtypeStruct(tokens.shape, BF16),
+            jax.ShapeDtypeStruct(tokens.shape, BF16),
+            jax.ShapeDtypeStruct((3, 4, INNER), BF16),
+            jax.ShapeDtypeStruct((4, INNER), BF16),
+            jax.ShapeDtypeStruct((4, 2, HID), BF16),
+            jax.ShapeDtypeStruct((4, HID), BF16),
+        ],
+        in_specs=[vmem] * 6,
+        out_specs=[vmem] * 6,
+    )(out, grad_input, gdown, gup, goq, gkv)
+    return out, grad_input, jnp.transpose(grad_qkv, (1, 0, 2)), grad_out_t, grad_up, grad_down_t
 
 
 def solution(mesh):

time: 93.6 us -> 73.2 us (0.78)
  the two profiles are of different devices: /device:TPU:1 before, /device:TPU:8 now
where the time goes in v2:
time: 73.2 us; the launch traced here: 73 us
  Pallas kernels  72.3 us (99%)
    pallas_call x1, Pallas kernels, shards(): pl.pallas_call(kernel, out_shape=out_shape, in_specs=[vmem] * 4 + [pl.Blo...  70.6 us
    pallas_call x1, Pallas kernels, shards(): pl.pallas_call(laid_out, out_shape=[jax.ShapeDtypeStruct(tokens.shape, BF...  1.71 us

profile of v2, /device:TPU:8, one launch (start us, length us, event | category | flops | bytes accessed | tf_op | source)
XLA Modules:
  0.0 73.0 jit_solution(6229915493341811401)
XLA Ops:
  0.6 70.6 %shard_map.136 = (bf16[8,16,512]{2,1,0:T(8,128)(2,1)}, bf16[8,16,512]{2,1,0:T(8,128)(2,1)}, bf16[4,1024]{1,0:T(4,128)(2,1)}, bf16[4,2048]{1,0:T(4,128)(2,1)}, bf...) custom-call(bf16[8,16,512]{2,1,0:T(8,128)(2,1)} %refs_0_.1, bf16[8,16,512]{2,1,0:T(8,128)(2,1)} %refs_1_.1, ...), custom_call_target="tpu_custom_call" | custom-call | tf_op jit(solution)/shard_map/pallas_call | solution.py:671
  71.3 1.7 %shard_map.137 = (bf16[8,16,512]{2,1,0:T(8,128)(2,1)}, bf16[8,16,512]{2,1,0:T(8,128)(2,1)}, bf16[3,4,256]{2,1,0:T(4,128)(2,1)}, bf16[4,256]{1,0:T(4,128)(2,1)}, ...) custom-call(bf16[8,16,512]{2,1,0:T(8,128)(2,1)} %get-tuple-element.18.out, ...), custom_call_target="tpu_custom_call" | custom-call | tf_op jit(solution)/shard_map/pallas_call | solution.py:693

commit v3 on v2

--- a/solution.py
+++ b/solution.py
@@ -321,11 +321,10 @@
 
     loads = []
     for i, (src, dst) in enumerate(
-        ((wqkv_h, wqkv), (wdown_h, wdown), (wout_h, wout), (wup_h, wup_pairs))
+        ((wqkv_h, wqkv), (wup_h, wup_pairs), (wdown_h, wdown), (wout_h, wout))
     ):
-        load = pltpu.make_async_copy(src, dst, local_sem.at[i])
-        load.start()
-        loads.append(load)
+        loads.append(pltpu.make_async_copy(src, dst, local_sem.at[i]))
+    loads[0].start()
 
     barrier = pltpu.get_barrier_semaphore()
     peers = [left, right, twin] + row_peer[1:] + z_peer[1:]
@@ -356,6 +355,8 @@
     ain[...] = a
     fgrad[...] = to_halves(gout[...].astype(F32)).astype(BF16)
     loads[0].wait()
+    for load in loads[1:]:
+        load.start()
     key_raw = nn(a, wqkv[1])
     key_norm = lax.rsqrt(head_sum(key_raw * key_raw) + EPS)
     keys = (key_raw * key_norm).astype(BF16)
@@ -414,17 +415,35 @@
 
     lax.fori_loop(0, 4, bias_rows, 0)
 
-    loads[3].wait()
-
     def part_rows(i, carry):
-        rows = pl.ds(pl.multiple_of(i * 16, 16), 16)
-        both = wup_pairs[rows].astype(F32)
-        wup[rows, :HID] = both[:, 0, :].astype(BF16)
-        wup[rows, HID:] = both[:, 1, :].astype(BF16)
+        rows = pl.ds(pl.multiple_of(i * 32, 32), 32)
+        both = wup_pairs[rows]
+        wup[rows, :HID] = both[:, 0, :]
+        wup[rows, HID:] = both[:, 1, :]
         return carry
 
-    lax.fori_loop(0, WIDTH // 16, part_rows, 0)
-
+    loads[1].wait()
+    lax.fori_loop(0, 8, part_rows, 0)
+    for copy in key_vert:
+        copy.wait_recv()
+    key_side += horizontal(0, 0) + horizontal(0, 2)
+    lax.fori_loop(8, 16, part_rows, 0)
+    for copy in key_side:
+        copy.wait_recv()
+
+    key_window = win[0].reshape(KEYS, INNER)
+    probs[...] = nt(qmask[...], key_window)
+    for copy in value_vert:
+        copy.wait_recv()
+    value_side += horizontal(1, 0) + horizontal(1, 2)
+
+    for i in range(16):
+        rows = pl.ds(i * 32, 32)
+        s = probs[rows, :] + bias[pl.ds((i % 4) * 32, 32), :]
+        e = jnp.exp(s - jnp.max(s, axis=-1, keepdims=True))
+        p = e * (1.0 / jnp.sum(e, axis=-1, keepdims=True))
+        probs[rows, :] = p
+        plow[rows, :] = p.astype(BF16)
     at = lax.broadcasted_iota(jnp.int32, (WIDTH, WIDTH), 0)
     of = lax.broadcasted_iota(jnp.int32, (WIDTH, WIDTH), 1)
     to = ((of >> 2) & 1) * 256 + (of >> 3) * 4 + (of & 3)
@@ -432,32 +451,10 @@
     left_t[0] = nt(order[...], fgrad[...]).astype(BF16)
     left_t[1] = nt(order[...], ain[...]).astype(BF16)
 
-    loads[1].wait()
     loads[2].wait()
+    loads[3].wait()
     ghid[...] = nt(fgrad[...], wdown[...])
 
-    for copy in key_vert:
-        copy.wait_recv()
-    key_side += horizontal(0, 0) + horizontal(0, 2)
-    for copy in value_vert:
-        copy.wait_recv()
-    value_side += horizontal(1, 0) + horizontal(1, 2)
-    for copy in key_side:
-        copy.wait_recv()
-
-    key_window = win[0].reshape(KEYS, INNER)
-    probs[...] = nt(qmask[...], key_window)
-
-    def softmax_rows(i, carry):
-        rows = pl.ds(pl.multiple_of(i * 32, 32), 32)
-        s = probs[rows, :] + bias[pl.ds(pl.multiple_of((i % 4) * 32, 32), 32), :]
-        e = jnp.exp(s - jnp.max(s, axis=-1, keepdims=True))
-        p = e * (1.0 / jnp.sum(e, axis=-1, keepdims=True))
-        probs[rows, :] = p
-        plow[rows, :] = p.astype(BF16)
-        return carry
-
-    lax.fori_loop(0, 16, softmax_rows, 0)
     for copy in value_side:
         copy.wait_recv()
     value_window = win[1].reshape(KEYS, INNER)
@@ -471,15 +468,20 @@
     attended = fold_heads(nn(plow[...], value_window)).astype(BF16)
     att[...] = attended
 
-    def exchange(slot, value):
-        sums[slot] = value.astype(BF16)
-        return links.start(sums.at[slot], sums_in.at[slot], twin)
-
-    def total_of(slot, copy):
-        copy.wait_recv()
-        return sums[slot].astype(F32) + sums_in[slot].astype(F32)
-
-    attn_sum = exchange(0, nn(attended, wout[...]))
+    def exchange(slot, product):
+        copies = []
+        for half in range(2):
+            sums[slot, half] = product(slice(half * INNER, (half + 1) * INNER)).astype(BF16)
+            copies.append(links.start(sums.at[slot, half], sums_in.at[slot, half], twin))
+        return copies
+
+    def total_of(slot, copies):
+        for copy in copies:
+            copy.wait_recv()
+        halves = [sums[slot, i].astype(F32) + sums_in[slot, i].astype(F32) for i in range(2)]
+        return jnp.concatenate(halves, axis=1)
+
+    attn_sum = exchange(0, lambda c: nn(attended, wout[:, c]))
     residual = to_halves(tok[...].astype(F32)) + total_of(0, attn_sum)
     resid[...] = residual
     m = (residual * norm_scale(residual) * mlp_gain[...]).astype(BF16)
@@ -497,8 +499,7 @@
         gh = ghid[:, cols]
         gmix[:, cols] = (gh * val * (cdf + gate * density)).astype(BF16)
         gmix[:, cols_v] = (gh * act).astype(BF16)
-    mlp_back = exchange(1, nt(gmix[...], wup[...]))
-    mlp_sum = exchange(2, nn(hidden[...], wdown[...]))
+    mlp_back = exchange(1, lambda c: nt(gmix[...], wup[c, :]))
 
     down_p.fill(left_t.at[0], hidden[...])
     down_p.core()
@@ -515,8 +516,6 @@
     grad_att = nt(grad_low, wout[...]).astype(BF16)
     for h, part in enumerate(head_rows(grad_att)):
         gmask[h * TOK : (h + 1) * TOK, :] = part
-
-    up_p.x1()
 
     def rims(kv, whole):
         whole = whole.reshape(4, 3, HALF, INNER)
@@ -529,18 +528,18 @@
         ]
 
     value_rims = rims(1, tn(plow[...], gmask[...]))
-    down_p.x2()
+    up_p.x1()
+    mlp_sum = exchange(2, lambda c: nn(hidden[...], wdown[:, c]))
     dprob[...] = nt(gmask[...], win[1].reshape(KEYS, INNER))
 
-    def score_rows(i, carry):
-        rows = pl.ds(pl.multiple_of(i * 32, 32), 32)
+    for i in range(16):
+        rows = pl.ds(i * 32, 32)
         p, g = probs[rows, :], dprob[rows, :]
         delta = jnp.sum(p * g, axis=-1, keepdims=True)
         dscore[rows, :] = (p * (g - delta)).astype(BF16)
-        return carry
-
-    lax.fori_loop(0, 16, score_rows, 0)
+
     key_rims = rims(0, tn(dscore[...], qmask[...]))
+    down_p.x2()
 
     def through_norm(which, incoming, factor):
         v, r = raw[2 * which], raw[2 * which + 1]
@@ -553,7 +552,6 @@
     oq_p.fill(left_t.at[3], att[...])
     oq_p.fill(left_t.at[1], gproj[:, :INNER], INNER)
     oq_p.core()
-    up_p.x2()
 
     def turn(kv, copies):
         for copy in copies:
@@ -569,6 +567,7 @@
 
     value_turn = turn(1, value_rims)
     key_turn = turn(0, key_rims)
+    up_p.x2()
     down_p.y()
     out_o[...] = from_halves(resid[...] + total_of(2, mlp_sum)).astype(BF16)
     oq_p.x1()
@@ -581,22 +580,27 @@
 
     gproj[:, 2 * INNER :] = owned(1, value_turn).astype(BF16)
     gproj[:, INNER : 2 * INNER] = through_norm(1, owned(0, key_turn), 1.0).astype(BF16)
-    back = nt(gproj[:, :INNER], wqkv[0]) + nt(gproj[:, INNER : 2 * INNER], wqkv[1])
-    in_back = exchange(3, back + nt(gproj[:, 2 * INNER :], wqkv[2]))
     kv_p.fill(left_t.at[1], gproj[:, INNER:])
     kv_p.core()
+
+    def in_part(c):
+        part = nt(gproj[:, :INNER], wqkv[0, c, :])
+        part = part + nt(gproj[:, INNER : 2 * INNER], wqkv[1, c, :])
+        return part + nt(gproj[:, 2 * INNER :], wqkv[2, c, :])
+
+    in_back = exchange(3, in_part)
     up_p.y()
     oq_p.x2()
+    kv_p.rows()
     down_p.z()
-    kv_p.rows()
     oq_p.y()
     grad_in = gresid[...] + norm_back(
         to_halves(tok[...].astype(F32)), attn_gain[...], total_of(3, in_back)
     )
     gin_o[...] = from_halves(grad_in).astype(BF16)
     up_p.z()
+    kv_p.z()
     oq_p.z()
-    kv_p.z()
     down_p.store()
     up_p.store()
     oq_p.store()
@@ -657,8 +661,8 @@
         pltpu.VMEM((TOK, HID), BF16),
         pltpu.VMEM((TOK, 2 * HID), BF16),
         pltpu.VMEM((TOK, 3 * INNER), BF16),
-        pltpu.VMEM((4, TOK, WIDTH), BF16),
-        pltpu.VMEM((4, TOK, WIDTH), BF16),
+        pltpu.VMEM((4, 2, TOK, INNER), BF16),
+        pltpu.VMEM((4, 2, TOK, INNER), BF16),
         pltpu.VMEM((2, 2, 3, HALF, INNER), F32),
         pltpu.VMEM((2, 2, 3, HALF, INNER), BF16),
         pltpu.VMEM((2, 2, 3, HALF, INNER), BF16),

time: 73.2 us -> 70.5 us (0.963)
  Pallas kernels: 72.3 us -> 69.7 us
    pallas_call x1, Pallas kernels: 70.6 us -> 68 us  [shards(): pl.pallas_call(kernel, out_shape=out_shape, in_specs=[vmem] * 4 + [pl.Blo...]
where the time goes in v3:
time: 70.5 us; the launch traced here: 70.4 us
  Pallas kernels  69.7 us (99%)
    pallas_call x1, Pallas kernels, shards(): pl.pallas_call(kernel, out_shape=out_shape, in_specs=[vmem] * 4 + [pl.Blo...  68 us
    pallas_call x1, Pallas kernels, shards(): pl.pallas_call(laid_out, out_shape=[jax.ShapeDtypeStruct(tokens.shape, BF...  1.71 us

profile of v3, /device:TPU:8, one launch (start us, length us, event | category | flops | bytes accessed | tf_op | source)
XLA Modules:
  0.0 70.4 jit_solution(4917081142258190709)
XLA Ops:
  0.6 68.0 %shard_map.136 = (bf16[8,16,512]{2,1,0:T(8,128)(2,1)}, bf16[8,16,512]{2,1,0:T(8,128)(2,1)}, bf16[4,1024]{1,0:T(4,128)(2,1)}, bf16[4,2048]{1,0:T(4,128)(2,1)}, bf...) custom-call(bf16[8,16,512]{2,1,0:T(8,128)(2,1)} %refs_0_.1, bf16[8,16,512]{2,1,0:T(8,128)(2,1)} %refs_1_.1, ...), custom_call_target="tpu_custom_call" | custom-call | tf_op jit(solution)/shard_map/pallas_call | solution.py:675
  68.6 1.7 %shard_map.137 = (bf16[8,16,512]{2,1,0:T(8,128)(2,1)}, bf16[8,16,512]{2,1,0:T(8,128)(2,1)}, bf16[3,4,256]{2,1,0:T(4,128)(2,1)}, bf16[4,256]{1,0:T(4,128)(2,1)}, ...) custom-call(bf16[8,16,512]{2,1,0:T(8,128)(2,1)} %get-tuple-element.18.out, ...), custom_call_target="tpu_custom_call" | custom-call | tf_op jit(solution)/shard_map/pallas_call | solution.py:697

commit v4 on v3

--- a/solution.py
+++ b/solution.py
@@ -134,7 +134,7 @@
             self.s2[side] = total.astype(BF16)
             self.copies.append(self.links.start(self.s2.at[side], self.r2.at[side], peer))
 
-    def y(self):
+    def z(self):
         p = self.place
         for copy in self.copies:
             copy.wait_recv()
@@ -142,25 +142,8 @@
         for side in range(2):
             total = self.xs[side, p["x"]].astype(F32) + self.r1[side, 0].astype(F32)
             total = (total + self.r2[side].astype(F32)).astype(BF16)
-            for half in range(2):
-                self.ys[half, :, side * wide : (side + 1) * wide] = total[
-                    half * 32 : half * 32 + 32
-                ]
-        self.copy = self.links.start(self.ys.at[1 - p["y"]], self.ry, p["y_peer"])
-
-    def z(self):
-        self.copy.wait_recv()
-        self.z_of(self.ys[self.place["y"]].astype(F32) + self.ry[...].astype(F32))
-
-    def z_of(self, total):
-        p = self.place
-        wide = total.shape[1] // 4
-        for k in range(NZ):
-            rows = total[4 * k : 4 * k + 4]
-            block = jnp.concatenate(
-                [rows[:, q * wide : (q + 1) * wide] for q in range(4)], axis=0
-            )
-            self.zs[k] = block.astype(BF16)
+            for k in range(NZ):
+                self.zs[k, side * 8 : side * 8 + 8, :] = total[8 * k : 8 * k + 8]
         self.copies = [
             self.links.start(
                 self.zs.at[lax.rem(p["z"] + d, NZ)], self.rz.at[d - 1], p["z_peer"][d]
@@ -168,13 +151,28 @@
             for d in range(1, NZ)
         ]
 
-    def store(self):
+    def y(self):
         p = self.place
         for copy in self.copies:
             copy.wait_recv()
         total = self.zs[p["z"]].astype(F32)
         for d in range(NZ - 1):
             total = total + self.rz[d].astype(F32)
+        wide = total.shape[1] // 2
+        for k in range(2):
+            quarters = [
+                total[8 * h + 4 * k : 8 * h + 4 * k + 4, q * wide : (q + 1) * wide]
+                for h in range(2)
+                for q in range(2)
+            ]
+            self.ys[k] = jnp.concatenate(quarters, axis=0).astype(BF16)
+        self.copy = self.links.start(self.ys.at[1 - p["y"]], self.ry, p["y_peer"])
+
+    def store(self):
+        self.copy.wait_recv()
+        self.write(self.ys[self.place["y"]].astype(F32) + self.ry[...].astype(F32))
+
+    def write(self, total):
         wide = total.shape[1]
         for q in range(4):
             self.out[:, q * wide : (q + 1) * wide] = total[4 * q : 4 * q + 4].astype(BF16)
@@ -184,28 +182,65 @@
     def __init__(self, links, place, refs, out):
         self.links, self.place, self.out = links, place, out
         self.part, self.rc, self.xs, self.r1, self.zs, self.rz = refs
-
-    def rows(self):
+        self.core_copies, self.copies = [None, None], []
+
+    def core(self, k, left_t, right):
+        core = self.place["core"]
+        for c in range(2):
+            product = nn(left_t[c * 256 : (c + 1) * 256, :], right)
+            self.part[k, c] = product.astype(BF16)
+        self.core_copies[k] = self.links.start(
+            self.part.at[k, 1 - core], self.rc.at[k], self.place["core_peer"]
+        )
+
+    def x(self, k):
         p = self.place
-        self.copy.wait_recv()
-        for i in range(NROW):
-            rows = pl.ds(i * 32, 32)
-            total = self.part[p["core"], rows, :].astype(F32) + self.rc[rows, :].astype(F32)
-            self.xs[i] = total.astype(BF16)
-        self.copies = [
+        self.core_copies[k].wait_recv()
+        for i in range(NX):
+            rows = pl.ds(i * 64, 64)
+            total = self.part[k, p["core"], rows, :].astype(F32)
+            self.xs[k, i] = (total + self.rc[k, rows, :].astype(F32)).astype(BF16)
+        self.copies += [
             self.links.start(
-                self.xs.at[lax.rem(p["row"] + d, NROW)], self.r1.at[d - 1], p["row_peer"][d]
+                self.xs.at[k, lax.rem(p["x"] + d, NX)], self.r1.at[k, d - 1], p["x_peer"][d]
             )
-            for d in range(1, NROW)
+            for d in range(1, NX)
         ]
 
-    def z(self):
+    def zy(self):
+        p = self.place
         for copy in self.copies:
             copy.wait_recv()
-        total = self.xs[self.place["row"]].astype(F32)
-        for d in range(NROW - 1):
-            total = total + self.r1[d].astype(F32)
-        self.z_of(total)
+        totals = []
+        for k in range(2):
+            total = self.xs[k, p["x"]].astype(F32)
+            for d in range(NX - 1):
+                total = total + self.r1[k, d].astype(F32)
+            totals.append(total)
+        for block in range(2 * NZ):
+            quarters = [
+                total[4 * block : 4 * block + 4, q * 128 : (q + 1) * 128]
+                for total in totals
+                for q in range(2)
+            ]
+            self.zs[block] = jnp.concatenate(quarters, axis=0).astype(BF16)
+        self.copies = []
+        for d in range(1, 2 * NZ):
+            to_z, to_y = lax.rem(p["z"] + d // 2, NZ), lax.rem(p["y"] + d % 2, 2)
+            self.copies.append(
+                self.links.start(
+                    self.zs.at[to_z * 2 + to_y], self.rz.at[d - 1], p["zy_peer"][d]
+                )
+            )
+
+    def store(self):
+        p = self.place
+        for copy in self.copies:
+            copy.wait_recv()
+        total = self.zs[p["z"] * 2 + p["y"]].astype(F32)
+        for d in range(2 * NZ - 1):
+            total = total + self.rz[d].astype(F32)
+        self.write(total)
 
 
 PIECES = (1024, 2048, 512, 512)
@@ -219,27 +254,27 @@
         pltpu.VMEM((2, 2, 64, n // 2), BF16),
         pltpu.VMEM((2, 64, n // 2), BF16),
         pltpu.VMEM((2, 64, n // 2), BF16),
-        pltpu.VMEM((2, 32, n), BF16),
-        pltpu.VMEM((32, n), BF16),
-        pltpu.VMEM((NZ, 16, n // 4), BF16),
-        pltpu.VMEM((NZ - 1, 16, n // 4), BF16),
+        pltpu.VMEM((2, 16, n // 4), BF16),
+        pltpu.VMEM((16, n // 4), BF16),
+        pltpu.VMEM((NZ, 16, n // 2), BF16),
+        pltpu.VMEM((NZ - 1, 16, n // 2), BF16),
     ]
 
 
 def last_scratch(n):
     return [
-        pltpu.VMEM((2, 256, n), BF16),
-        pltpu.VMEM((256, n), BF16),
-        pltpu.VMEM((NROW, 32, n), BF16),
-        pltpu.VMEM((NROW - 1, 32, n), BF16),
-        pltpu.VMEM((NZ, 16, n // 4), BF16),
-        pltpu.VMEM((NZ - 1, 16, n // 4), BF16),
+        pltpu.VMEM((2, 2, 256, n // 2), BF16),
+        pltpu.VMEM((2, 256, n // 2), BF16),
+        pltpu.VMEM((2, NX, 64, n // 2), BF16),
+        pltpu.VMEM((2, NX - 1, 64, n // 2), BF16),
+        pltpu.VMEM((2 * NZ, 16, n // 4), BF16),
+        pltpu.VMEM((2 * NZ - 1, 16, n // 4), BF16),
     ]
 
 
 PER_PIECE = 10
 PER_LAST = 6
-MESSAGES = 96
+MESSAGES = 104
 
 
 def kernel(*refs):
@@ -297,10 +332,13 @@
     right = (row, lax.rem(col + 1, NCOL), ch)
     twin = (row, col, 1 - ch)
     x_flip = x + 1 - 2 * lax.rem(x, 2)
-    row_peer = [(lax.rem(row + d, NROW), col, ch) for d in range(NROW)]
+    x_peer = [(lax.rem(x + d, NX) * 2 + y, col, ch) for d in range(NX)]
     z_peer = [(row, lax.rem(z + d, NZ) * 2 + core, ch) for d in range(NZ)]
+    zy_peer = [
+        (x * 2 + lax.rem(y + d % 2, 2), lax.rem(z + d // 2, NZ) * 2 + core, ch)
+        for d in range(2 * NZ)
+    ]
     place = {
-        "row": row,
         "x": x,
         "y": y,
         "z": z,
@@ -311,7 +349,8 @@
         "x_far_peer": ((NX - 1 - x) * 2 + y, col, ch),
         "core_peer": (row, z * 2 + 1 - core, ch),
         "y_peer": (x * 2 + 1 - y, col, ch),
-        "row_peer": row_peer,
+        "x_peer": x_peer,
+        "zy_peer": zy_peer,
         "z_peer": z_peer,
     }
     links = Links(send_sem, recv_sem)
@@ -327,7 +366,7 @@
     loads[0].start()
 
     barrier = pltpu.get_barrier_semaphore()
-    peers = [left, right, twin] + row_peer[1:] + z_peer[1:]
+    peers = [above, below, left, right, twin] + x_peer[1:] + zy_peer[2:]
     for peer in peers:
         pl.semaphore_signal(barrier, inc=1, device_id=peer, device_id_type=MESH)
 
@@ -446,7 +485,8 @@
         plow[rows, :] = p.astype(BF16)
     at = lax.broadcasted_iota(jnp.int32, (WIDTH, WIDTH), 0)
     of = lax.broadcasted_iota(jnp.int32, (WIDTH, WIDTH), 1)
-    to = ((of >> 2) & 1) * 256 + (of >> 3) * 4 + (of & 3)
+    to = ((of >> 2) & 1) * 256 + (of >> 7) * 64 + ((of >> 3) & 7) * 8
+    to = to + ((of >> 6) & 1) * 4 + (of & 3)
     order[...] = jnp.where(at == to, 1.0, 0.0).astype(BF16)
     left_t[0] = nt(order[...], fgrad[...]).astype(BF16)
     left_t[1] = nt(order[...], ain[...]).astype(BF16)
@@ -568,7 +608,7 @@
     value_turn = turn(1, value_rims)
     key_turn = turn(0, key_rims)
     up_p.x2()
-    down_p.y()
+    down_p.z()
     out_o[...] = from_halves(resid[...] + total_of(2, mlp_sum)).astype(BF16)
     oq_p.x1()
 
@@ -579,9 +619,9 @@
         return mine.reshape(TOK, INNER)
 
     gproj[:, 2 * INNER :] = owned(1, value_turn).astype(BF16)
+    kv_p.core(1, left_t.at[1], gproj[:, 2 * INNER :])
     gproj[:, INNER : 2 * INNER] = through_norm(1, owned(0, key_turn), 1.0).astype(BF16)
-    kv_p.fill(left_t.at[1], gproj[:, INNER:])
-    kv_p.core()
+    kv_p.core(0, left_t.at[1], gproj[:, INNER : 2 * INNER])
 
     def in_part(c):
         part = nt(gproj[:, :INNER], wqkv[0, c, :])
@@ -589,18 +629,19 @@
         return part + nt(gproj[:, 2 * INNER :], wqkv[2, c, :])
 
     in_back = exchange(3, in_part)
-    up_p.y()
+    kv_p.x(1)
+    up_p.z()
+    kv_p.x(0)
     oq_p.x2()
-    kv_p.rows()
-    down_p.z()
-    oq_p.y()
+    down_p.y()
     grad_in = gresid[...] + norm_back(
         to_halves(tok[...].astype(F32)), attn_gain[...], total_of(3, in_back)
     )
     gin_o[...] = from_halves(grad_in).astype(BF16)
-    up_p.z()
-    kv_p.z()
     oq_p.z()
+    kv_p.zy()
+    up_p.y()
+    oq_p.y()
     down_p.store()
     up_p.store()
     oq_p.store()

time: 70.5 us -> 69.5 us (0.986)
  Pallas kernels: 69.7 us -> 68.7 us
    pallas_call x1, Pallas kernels: 68 us -> 67 us  [shards(): pl.pallas_call(kernel, out_shape=out_shape, in_specs=[vmem] * 4 + [pl.Blo...]
where the time goes in v4:
time: 69.5 us; the launch traced here: 69.3 us
  Pallas kernels  68.7 us (99%)
    pallas_call x1, Pallas kernels, shards(): pl.pallas_call(kernel, out_shape=out_shape, in_specs=[vmem] * 4 + [pl.Blo...  67 us
    pallas_call x1, Pallas kernels, shards(): pl.pallas_call(laid_out, out_shape=[jax.ShapeDtypeStruct(tokens.shape, BF...  1.71 us

profile of v4, /device:TPU:8, one launch (start us, length us, event | category | flops | bytes accessed | tf_op | source)
XLA Modules:
  0.0 69.3 jit_solution(15241656936490797569)
XLA Ops:
  0.6 67.0 %shard_map.136 = (bf16[8,16,512]{2,1,0:T(8,128)(2,1)}, bf16[8,16,512]{2,1,0:T(8,128)(2,1)}, bf16[4,1024]{1,0:T(4,128)(2,1)}, bf16[4,2048]{1,0:T(4,128)(2,1)}, bf...) custom-call(bf16[8,16,512]{2,1,0:T(8,128)(2,1)} %refs_0_.1, bf16[8,16,512]{2,1,0:T(8,128)(2,1)} %refs_1_.1, ...), custom_call_target="tpu_custom_call" | custom-call | tf_op jit(solution)/shard_map/pallas_call | solution.py:716
  67.6 1.7 %shard_map.137 = (bf16[8,16,512]{2,1,0:T(8,128)(2,1)}, bf16[8,16,512]{2,1,0:T(8,128)(2,1)}, bf16[3,4,256]{2,1,0:T(4,128)(2,1)}, bf16[4,256]{1,0:T(4,128)(2,1)}, ...) custom-call(bf16[8,16,512]{2,1,0:T(8,128)(2,1)} %get-tuple-element.18.out, ...), custom_call_target="tpu_custom_call" | custom-call | tf_op jit(solution)/shard_map/pallas_call | solution.py:738
